TPU v7x, 32 devices: a whole 2x2x4 slice. The times are simulated.
32 devices in a mesh: grp: 4 (over y, x), wide: 8 (over z, core).
Axes of the slice: x: 2, y: 2, z: 4, core: 2. Of those that a mesh axis runs over, the one named last changes fastest.
Arguments:
- embeddings: float32 [49152, 768], P(('grp', 'wide')), may hold values from -200 to 200, as said below
Outputs:
- whitened: float32 [49152, 768], P(('grp', 'wide'))
- factor_scaled: float32 [768, 768], replicated
Inputs may be any that keep to these rules, and one draw needn't show every extreme that they name: `embeddings`: Real-valued rows; no structure is promised.
All inputs are finite; a program needn't handle non-finite values.
Results may differ from a plain program's by a relative error of at most 0.000054.
Values sent between devices are 32-bit elements; how exact they have to be, the bound alone decides.
No kernel may reach another device: no remote copies, remote signals or barrier semaphores. Data moves between devices by JAX's collectives and lax.ppermute only.
A program may use at most 128 MiB of HBM per device.

v0:
```python
import jax
import jax.numpy as jnp
from jax import lax
from jax.sharding import PartitionSpec as P


def self_product(rows):
    return lax.dot_general(
        rows,
        rows,
        (((0,), (0,)), ((), ())),
        precision=lax.Precision.HIGHEST,
        preferred_element_type=jnp.float32,
    )


def shards(embeddings):
    row_count = embeddings.shape[0] * lax.axis_size("grp") * lax.axis_size("wide")
    col_total = lax.psum(jnp.sum(embeddings, axis=0), ("grp", "wide"))
    col_mean = col_total / row_count
    centred = embeddings - col_mean[None, :]
    payload = lax.psum(self_product(centred), ("grp", "wide"))
    lower = jnp.linalg.cholesky(payload)
    factor = lower.T
    scale = jnp.sqrt(jnp.float32(row_count))
    solved = jax.scipy.linalg.solve_triangular(lower, centred.T, lower=True)
    whitened = solved.T * scale
    return (whitened, factor / scale)


def solution(mesh):
    placed = (P(("grp", "wide"), None),)
    return jax.shard_map(
        shards,
        mesh=mesh,
        in_specs=placed,
        out_specs=(P(("grp", "wide"), None), P()),
        check_vma=False,
    )
```

profile of v0, /device:TPU:0, one launch (start us, length us, event | category | flops | bytes accessed | tf_op | source)
XLA Modules:
  0.0 476.7 jit_solution(18385280048948252575)
XLA Ops:
  7.2 2.7 reduce_sum.9
  9.9 42.0 %psum.14 = f32[768]{0:T(1024)S(1)} all-reduce(f32[768]{0:T(1024)S(1)} %reduce_sum.9), channel_id=1, replica_groups=mesh['grp'=4,'wide'=8] {'grp','wide'}, use_global_device_ids=true, to_apply=%region_1.0 | all-reduce | flops 768 | bytes 6144 | tf_op jit(solution)/shard_map/psum | solution.py:19
  51.9 16.3 %fusion = f32[768,768]{0,1:T(8,128)} fusion(f32[1536,768]{1,0:T(8,128)} %param.1, f32[768]{0:T(1024)S(1)} %broadcast_multiply_fusion), kind=kOutput, calls=%fused_computation.4 | convolution fusion | flops 10872815616 | bytes 7080960 | tf_op jit(solution)/shard_map/dot_general | solution.py:8
  68.3 4.8 %subtract_bitcast_fusion = f32[768,1536]{0,1:T(8,128)} fusion(f32[1536,768]{1,0:T(8,128)} %param.1, f32[768]{0:T(1024)S(1)} %broadcast_multiply_fusion), kind=kLoop, calls=%fused_computation.3 | loop fusion | flops 1179648 | bytes 9440256 | tf_op jit(solution)/shard_map/transpose | solution.py:26
  73.1 130.2 %all-reduce.3.cloned.1.call-done = f32[768,768]{0,1:T(8,128)} async-done(((f32[768,768]{0,1:T(8,128)}), f32[768,768]{0,1:T(8,128)}) %all-reduce.3.cloned.1.call-update) | async-done | bytes 2359312 | tf_op jit(solution)/shard_map/psum | solution.py:22
  203.3 3.4 copy.4
  210.1 11.7 %cholesky.165 = f32[128,128]{1,0:T(8,128)S(1)} custom-call(f32[128,128]{1,0:T(8,128)S(1)} %cholesky.424), custom_call_target="Cholesky" | custom-call | tf_op jit(solution)/shard_map/jit(cholesky)/cholesky | solution.py:23
  222.0 9.8 %custom-call.47 = f32[1,128,128]{1,2,0:T(8,128)S(1)} custom-call(f32[1,128,128]{2,1,0:T(8,128)S(1)} %get-tuple-element.49), custom_call_target="InvertDiagBlocksLowerTriangular" | custom-call | tf_op jit(solution)/shard_map/jit(cholesky)/cholesky | solution.py:23
  234.6 11.7 %cholesky.188 = f32[128,128]{1,0:T(8,128)S(1)} custom-call(f32[128,128]{1,0:T(8,128)S(1)} %cholesky.428), custom_call_target="Cholesky" | custom-call | tf_op jit(solution)/shard_map/jit(cholesky)/cholesky | solution.py:23
  246.4 10.2 %custom-call.48 = f32[1,128,128]{1,2,0:T(8,128)S(1)} custom-call(f32[1,128,128]{2,1,0:T(8,128)S(1)} %get-tuple-element.46), custom_call_target="InvertDiagBlocksLowerTriangular" | custom-call | tf_op jit(solution)/shard_map/jit(cholesky)/cholesky | solution.py:23
  258.5 11.7 %cholesky.354 = f32[128,128]{1,0:T(8,128)S(1)} custom-call(f32[128,128]{1,0:T(8,128)S(1)} %cholesky.433), custom_call_target="Cholesky" | custom-call | tf_op jit(solution)/shard_map/jit(cholesky)/cholesky | solution.py:23
  270.9 9.8 %custom-call.49 = f32[1,128,128]{1,2,0:T(8,128)S(1)} custom-call(f32[1,128,128]{2,1,0:T(8,128)S(1)} %get-tuple-element.43), custom_call_target="InvertDiagBlocksLowerTriangular" | custom-call | tf_op jit(solution)/shard_map/jit(cholesky)/cholesky | solution.py:23
  282.6 11.9 %cholesky.373 = f32[128,128]{1,0:T(8,128)S(1)} custom-call(f32[128,128]{1,0:T(8,128)S(1)} %cholesky.438), custom_call_target="Cholesky" | custom-call | tf_op jit(solution)/shard_map/jit(cholesky)/cholesky | solution.py:23
  295.2 9.8 %custom-call.50 = f32[1,128,128]{1,2,0:T(8,128)S(1)} custom-call(f32[1,128,128]{2,1,0:T(8,128)S(1)} %get-tuple-element.40), custom_call_target="InvertDiagBlocksLowerTriangular" | custom-call | tf_op jit(solution)/shard_map/jit(cholesky)/cholesky | solution.py:23
  306.8 11.7 %cholesky.392 = f32[128,128]{1,0:T(8,128)S(1)} custom-call(f32[128,128]{1,0:T(8,128)S(1)} %cholesky.443), custom_call_target="Cholesky" | custom-call | tf_op jit(solution)/shard_map/jit(cholesky)/cholesky | solution.py:23
  319.2 9.8 %custom-call.51 = f32[1,128,128]{1,2,0:T(8,128)S(1)} custom-call(f32[1,128,128]{2,1,0:T(8,128)S(1)} %get-tuple-element.37), custom_call_target="InvertDiagBlocksLowerTriangular" | custom-call | tf_op jit(solution)/shard_map/jit(cholesky)/cholesky | solution.py:23
  330.5 12.1 %cholesky.410 = f32[128,128]{1,0:T(8,128)S(1)} custom-call(f32[128,128]{1,0:T(8,128)S(1)} %convolution_subtract_fusion.8), custom_call_target="Cholesky" | custom-call | tf_op jit(solution)/shard_map/jit(cholesky)/cholesky | solution.py:23
  347.8 2.5 multiply_bitcast_fusion.1
  350.3 3.1 copy.6
  353.4 16.7 %while.1 = (s32[]{:T(128)}, f32[768,768]{1,0:T(8,128)}, s32[6,2]{0,1:T(2,128)S(1)}, f32[6,128,128]{2,1,0:T(8,128)S(1)}, s32[]{:T(128)}) while((s32[]{:T(128)}, f32[768,768]{1,0:T(8,128)}, s32[6,2]{0,1:T(2,128)S(1)}, f32[6,128,128]{2,1,0:T(8,128)S(1)}, s32[]{:T(128)}) %tuple.46), condition=%wide.while_cond, body=%wide.while_body.sunk | while | flops 2 | bytes 131189 | solution.py:26
  354.0 2.2 bitcast_dynamic-update-slice_fusion.2
  356.8 2.2 bitcast_dynamic-update-slice_fusion.2
  359.6 2.2 bitcast_dynamic-update-slice_fusion.2
  362.4 2.2 bitcast_dynamic-update-slice_fusion.2
  370.1 59.0 %custom-call.52 = f32[6,128,128]{1,2,0:T(8,128)S(1)} custom-call(f32[6,128,128]{2,1,0:T(8,128)S(1)} %get-tuple-element.9), custom_call_target="InvertDiagBlocksLowerTriangular" | custom-call | tf_op jit(solution)/shard_map/jit(_solve_triangular)/triangular_solve | solution.py:26
  431.3 2.6 convolution_subtract_fusion.3
  434.9 3.6 convolution_subtract_fusion
  439.4 5.0 %convolution_subtract_fusion.2 = f32[128,1536]{0,1:T(8,128)S(1)} fusion(f32[128,1536]{1,0:T(8,128)S(1)} %get-tuple-element.54, f32[128,1536]{1,0:T(8,128)S(1)} %get-tuple-element.53, f32[128,1536]{1,0:T(8,128)S(1)} %get-tuple-element.52, f32[768,1536]{0,1:T(8,128)S(1)} %bitcast.84, f32[768,768]{1,0:T(8,128)} %get-tuple-element.104), kind=kOutput, calls=%fused_computation.17 | convolution fusion | flops 907345920 | bytes 4128768 | tf_op jit(solution)/shard_map/jit(_solve_triangular)/triangular_solve | solution.py:26
  445.3 6.4 %fusion.10 = f32[128,1536]{0,1:T(8,128)S(1)} fusion(f32[128,1536]{1,0:T(8,128)S(1)} %get-tuple-element.55, f32[128,1536]{1,0:T(8,128)S(1)} %get-tuple-element.54, f32[128,1536]{1,0:T(8,128)S(1)} %get-tuple-element.53, f32[128,1536]{1,0:T(8,128)S(1)} %get-tuple-element.52, f32[768,1536]{0,1:T(8,128)S(1)} %bitcast.84, f32[768,768]{1,0:T(8,128)} %get-tuple-element.104), kind=kOutput, calls=%fused_computation.19 | convolution fusion | flops 1210515456 | bytes 4980736 | tf_op jit(solution)/shard_map/jit(_solve_triangular)/triangular_solve | solution.py:26
  452.6 7.5 %convolution_subtract_fusion.1 = f32[128,1536]{0,1:T(8,128)S(1)} fusion(f32[640,1536]{1,0:T(8,128)S(1)} %get-tuple-element.24, f32[768,1536]{0,1:T(8,128)S(1)} %bitcast.84, f32[768,768]{1,0:T(8,128)} %get-tuple-element.104), kind=kOutput, calls=%fused_computation.16 | convolution fusion | flops 1510146048 | bytes 5832704 | tf_op jit(solution)/shard_map/jit(_solve_triangular)/triangular_solve | solution.py:26
  461.0 2.6 multiply_bitcast_fusion
  463.6 6.0 %copy.5 = f32[1536,768]{1,0:T(8,128)} copy(f32[1536,768]{0,1:T(8,128)} %multiply_bitcast_fusion) | data formatting | bytes 9437184
  (63 shorter events, 31.6 us)
Async XLA Ops:
  7.2 196.1 %all-reduce.3.cloned.1.call-start = ((), (), s32[]{:S(2)}) async-start(), calls=%async_computation | async-start | bytes 4718592 | tf_op jit(solution)/shard_map/psum | solution.py:22
  203.3 3.4 copy-start
  208.7 1.4 copy-start.1
  350.3 84.5 %slice-start = ((s8[4718592]{0:T(1024)(128)(4,1)}), s8[524288]{0:T(1024)(128)(4,1)S(1)}, s32[]{:S(2)}) async-start(s8[4718592]{0:T(1024)(128)(4,1)} %bitcast.83), calls=%async_computation.1 | async-start | bytes 1048576
  429.1 5.7 %slice-start.1 = ((s8[4718592]{0:T(1024)(128)(4,1)}), s8[4194304]{0:T(1024)(128)(4,1)S(1)}, s32[]{:S(2)}) async-start(s8[4718592]{0:T(1024)(128)(4,1)} %bitcast.83), calls=%async_computation.2 | async-start | bytes 8388608
Sparse Core Ops, SparseCore 0:
  68.4 134.8 all-reduce.2
where the time goes:
time: 484 us; the launch traced here: 477 us
  other arithmetic  197 us (41%)
  waiting for transfers between devices  130 us (27%)
  matrix products  57.9 us (12%)
  blocking collectives  42 us (9%)
  local copies, waits for them, and re-layouts  30.8 us (6%)
  between operations  18.3 us (4%)
    psum x1, waiting for transfers between devices, shards(): payload = lax.psum(self_product(centred), ('grp', 'wide'))  130 us
    another operation x22, other arithmetic, shards(): lower = jnp.linalg.cholesky(payload)  124 us
    another operation x2, other arithmetic, shards(): solved = jax.scipy.linalg.solve_triangular(lower, centred.T, lower=True)  59 us
    psum x1, blocking collectives, shards(): col_total = lax.psum(jnp.sum(embeddings, axis=0), ('grp', 'wide'))  42 us
    another operation x11, matrix products, shards(): solved = jax.scipy.linalg.solve_triangular(lower, centred.T, lower=True)  31.7 us
    another operation x18, local copies, waits for them, and re-layouts  16.6 us
    dot_general x1, matrix products, self_product(): lax.dot_general(rows, rows, (((0,), (0,)), ((), ())), precision=lax.Preci...  16.3 us
    unnamed x10, local copies, waits for them, and re-layouts  10.6 us
  transfers between devices with their start and end apart: 1, of which 1 were waited for; matrix products, arithmetic and copies ran while one was open for 1% of the time, Pallas kernels for 0%

commit v1 on v0

v1 whole, which is shorter than its diff:
```python
import jax
import jax.numpy as jnp
from jax import lax
from jax.experimental import pallas as pl
from jax.experimental.pallas import tpu as pltpu
from jax.sharding import PartitionSpec as P

AXES = ("grp", "wide")
LANES = 128
SUB = 8
HIGHEST = lax.Precision.HIGHEST


def dot(a, b, dims):
    return lax.dot_general(
        a, b, (dims, ((), ())), precision=HIGHEST, preferred_element_type=jnp.float32
    )


def over_lanes(tile, lane):
    return jnp.broadcast_to(tile[:, lane : lane + 1], (SUB, LANES))


def over_rows(tile, row):
    return jnp.broadcast_to(tile[row : row + 1, :], (SUB, LANES))


def factor_block(block, upper_ref, inverse_ref):
    groups = LANES // SUB
    tiles = [block[SUB * p : SUB * (p + 1), :] for p in range(groups)]
    row_at = lax.broadcasted_iota(jnp.int32, (SUB, LANES), 0)
    lane_at = lax.broadcasted_iota(jnp.int32, (SUB, LANES), 1)
    unit = [
        jnp.where(lane_at == row_at + SUB * p, 1.0, 0.0).astype(jnp.float32)
        for p in range(groups)
    ]
    for g in range(groups):
        base = SUB * g
        rows = [over_rows(tiles[g], i) for i in range(SUB)]
        carried = [over_rows(unit[g], i) for i in range(SUB)]
        s = {
            (i, j): over_lanes(rows[i], base + j) for i in range(SUB) for j in range(i, SUB)
        }
        scale = []
        for j in range(SUB):
            r = lax.rsqrt(s[j, j])
            scale.append(r)
            rows[j] = rows[j] * r
            carried[j] = carried[j] * r
            for k in range(j + 1, SUB):
                s[j, k] = s[j, k] * r
            for k in range(j + 1, SUB):
                for m in range(k, SUB):
                    s[k, m] = s[k, m] - s[j, k] * s[j, m]
                rows[k] = rows[k] - s[j, k] * rows[j]
                carried[k] = carried[k] - s[j, k] * carried[j]
            upper_ref[base + j : base + j + 1, :] = rows[j][:1, :]
            inverse_ref[base + j : base + j + 1, :] = carried[j][:1, :]
        if g == groups - 1:
            break
        for i in reversed(range(SUB)):
            for k in range(i + 1, SUB):
                rows[i] = rows[i] - s[i, k] * rows[k]
                carried[i] = carried[i] - s[i, k] * carried[k]
            rows[i] = rows[i] * scale[i]
            carried[i] = carried[i] * scale[i]
        for p in range(g + 1, groups):
            column = [over_lanes(tiles[p], base + i) for i in range(SUB)]
            tiles[p] = tiles[p] - sum(c * x for c, x in zip(column, rows))
            unit[p] = unit[p] - sum(c * x for c, x in zip(column, carried))


def factor_kernel(gram_ref, means_ref, count_ref, factor_ref, inverse_ref, work, upper, inverse):
    width = gram_ref.shape[0]
    blocks = width // LANES
    means = means_ref[...]
    apart = means - jnp.mean(means, axis=0, keepdims=True)
    between = dot(apart, apart, ((0,), (0,)))
    work[...] = gram_ref[...] + between * count_ref[0]
    total_scale = count_ref[1]
    row_at = lax.broadcasted_iota(jnp.int32, (LANES, width), 0)
    col_at = lax.broadcasted_iota(jnp.int32, (LANES, width), 1)

    def stage(k, _):
        start = pl.multiple_of(k * LANES, LANES)
        here = pl.ds(start, LANES)
        factor_block(work[here, here], upper, inverse)
        solved = dot(inverse[...], work[here, :], ((1,), (0,)))
        work[here, :] = solved
        work[here, here] = upper[...]
        factor_ref[here, :] = jnp.where(
            col_at >= row_at + start, work[here, :] * (1.0 / total_scale), 0.0
        )
        work[here, here] = inverse[...]
        inverse_ref[here, :] = jnp.where(
            col_at <= row_at + start, work[here, :] * total_scale, 0.0
        )

        def below(i, _):
            there = pl.ds(pl.multiple_of(i * LANES, LANES), LANES)
            work[there, here] = jnp.zeros((LANES, LANES), jnp.float32)
            work[there, :] = work[there, :] - dot(
                work[here, there], work[here, :], ((0,), (0,))
            )
            return 0

        lax.fori_loop(k + 1, blocks, below, 0)
        return 0

    lax.fori_loop(0, blocks, stage, 0)


def factor_and_inverse(gram, means, local_rows, row_count):
    width = gram.shape[0]
    square = jax.ShapeDtypeStruct((width, width), jnp.float32)
    counts = jnp.array([local_rows, row_count**0.5], jnp.float32)
    return pl.pallas_call(
        factor_kernel,
        out_shape=(square, square),
        in_specs=[
            pl.BlockSpec(memory_space=pltpu.VMEM),
            pl.BlockSpec(memory_space=pltpu.VMEM),
            pl.BlockSpec(memory_space=pltpu.SMEM),
        ],
        out_specs=(pl.BlockSpec(memory_space=pltpu.VMEM),) * 2,
        scratch_shapes=[
            pltpu.VMEM((width, width), jnp.float32),
            pltpu.VMEM((LANES, LANES), jnp.float32),
            pltpu.VMEM((LANES, LANES), jnp.float32),
        ],
        compiler_params=pltpu.CompilerParams(vmem_limit_bytes=40 * 2**20),
    )(gram, means, counts)


def shards(embeddings):
    local_rows, width = embeddings.shape
    devices = lax.axis_size("grp") * lax.axis_size("wide")
    row_count = local_rows * devices
    me = lax.axis_index(AXES)
    mean = jnp.sum(embeddings, axis=0, keepdims=True) / local_rows
    centred = embeddings - mean
    gram = dot(centred, centred, ((0,), (0,)))
    mine = lax.broadcasted_iota(jnp.int32, (devices, 1), 0) == me
    payload = jnp.concatenate([gram, jnp.where(mine, mean, 0.0)], axis=0)
    payload = lax.psum(payload, AXES)
    means = payload[width:]
    factor, inverse = factor_and_inverse(payload[:width], means, local_rows, row_count)
    col_mean = jnp.mean(means, axis=0, keepdims=True)
    whitened = dot(embeddings - col_mean, inverse, ((1,), (1,)))
    return (whitened, factor)


def solution(mesh):
    rows = P(AXES, None)
    return jax.shard_map(
        shards,
        mesh=mesh,
        in_specs=(rows,),
        out_specs=(rows, P()),
        check_vma=False,
    )
```

time: 484 us -> 238 us (0.49); the launches traced: 477 us -> 238 us
  other arithmetic: 197 us -> 5.29 us
  Pallas kernels: 0 us -> 49.9 us
  blocking collectives: 42 us -> 0 us
  matrix products: 57.9 us -> 28.8 us
  local copies, waits for them, and re-layouts: 30.8 us -> 1.98 us
  waiting for transfers between devices: 130 us -> 138 us
    another operation x24 -> x0, other arithmetic: 183 us -> none  [the longest x22 124 us: shards(): lower = jnp.linalg.cholesky(payload)]
    pallas_call x0 -> x1, Pallas kernels: none -> 49.9 us  [factor_and_inverse(): pl.pallas_call(factor_kernel, out_shape=(square, square), in_specs=[pl.Bl...]
    psum x1 -> x0, blocking collectives: 42 us -> none  [shards(): col_total = lax.psum(jnp.sum(embeddings, axis=0), ('grp', 'wide'))]
    another operation x21 -> x0, matrix products: 41.5 us -> none  [the longest x11 31.7 us: shards(): solved = jax.scipy.linalg.solve_triangular(lower, centred.T, lower=True)]
    another operation x25 -> x0, local copies, waits for them, and re-layouts: 16.8 us -> none
    dot_general x1 -> x2, matrix products: 16.3 us -> 28.8 us  [dot(): lax.dot_general(a, b, (dims, ((), ())), precision=HIGHEST, preferred_elem...]
    unnamed x10 -> x4, local copies, waits for them, and re-layouts: 10.6 us -> 0.01 us
    psum x1, waiting for transfers between devices: 130 us -> 138 us  [shards(): payload = lax.psum(payload, AXES)]
  transfers between devices with their start and end apart: 1 -> 1, of which waited for: 1 -> 1; matrix products, arithmetic and copies ran while one was open for 1% -> 0% of each run, Pallas kernels for 0% -> 0%
where the time goes in v1:
time: 238 us
  waiting for transfers between devices  138 us (58%)
  Pallas kernels  49.9 us (21%)
  matrix products  28.8 us (12%)
  between operations  14.1 us (6%)
  other arithmetic  5.29 us (2%)
    psum x1, waiting for transfers between devices, shards(): payload = lax.psum(payload, AXES)  138 us
    pallas_call x1, Pallas kernels, factor_and_inverse(): pl.pallas_call(factor_kernel, out_shape=(square, square), in_specs=[pl.Bl...  49.9 us
    dot_general x2, matrix products, dot(): lax.dot_general(a, b, (dims, ((), ())), precision=HIGHEST, preferred_elem...  28.8 us
  transfers between devices with their start and end apart: 1, of which 1 were waited for; matrix products, arithmetic and copies ran while one was open for 0% of the time, Pallas kernels for 0%

profile of v1, /device:TPU:0, one launch (start us, length us, event | category | flops | bytes accessed | tf_op | source)
XLA Modules:
  0.0 238.2 jit_solution(16098031086020136030)
XLA Ops:
  7.2 0.0 all-reduce.2.cloned.1.call-start
  7.2 2.7 %reduce_sum.18 = f32[768]{0:T(1024)S(1)} reduce(f32[1536,768]{1,0:T(8,128)} %param.2, f32[]{:T(128)} %constant.7.clone.1), dimensions={0}, to_apply=%region_0.0 | reduce | flops 1178880 | bytes 4721668 | tf_op jit(solution)/shard_map/reduce_sum | solution.py:140
  9.9 15.7 %fusion.2 = f32[768,768]{1,0:T(8,128)S(1)} fusion(f32[1536,768]{1,0:T(8,128)} %param.2, f32[768]{0:T(1024)S(1)} %broadcast_multiply_fusion.1), kind=kOutput, calls=%fused_computation.2 | convolution fusion | flops 10872815616 | bytes 7080960 | tf_op jit(solution)/shard_map/dot_general | solution.py:15
  25.6 0.1 broadcast_select_fusion
  25.7 1.6 pad_maximum_fusion
  27.3 0.0 all-reduce.2.cloned.1.call-update
  27.3 0.0 copy-start
  27.4 138.2 %all-reduce.2.cloned.1.call-done = f32[800,768]{1,0:T(8,128)} async-done(((f32[800,768]{1,0:T(8,128)}), f32[800,768]{1,0:T(8,128)}) %all-reduce.2.cloned.1.call-update) | async-done | bytes 2457616 | tf_op jit(solution)/shard_map/psum | solution.py:145
  165.5 0.9 slice_reduce_fusion
  166.4 0.0 copy-start.1
  166.4 2.0 slice.9.gram_ref
  168.4 0.0 copy-done
  168.4 49.9 %shard_map.41 = (f32[768,768]{1,0:T(8,128)}, f32[768,768]{1,0:T(8,128)S(1)}) custom-call(f32[768,768]{1,0:T(8,128)S(1)} %slice.9.gram_ref, f32[32,768]{1,0:T(8,128)S(1)} %get-tuple-element.7.means_ref, f32[2]{0:T(128)S(1)} %copy-done), custom_call_target="tpu_custom_call" | custom-call | tf_op jit(solution)/shard_map/pallas_call | solution.py:117
  218.3 0.0 copy-done.1
  218.3 13.1 %fusion = f32[1536,768]{1,0:T(8,128)} fusion(f32[768,768]{1,0:T(8,128)S(1)} %get-tuple-element.4, f32[1536,768]{1,0:T(8,128)S(1)} %copy-done.1, f32[768]{0:T(1024)S(1)} %broadcast_multiply_fusion), kind=kOutput, calls=%fused_computation | convolution fusion | flops 10872815616 | bytes 11799552 | tf_op jit(solution)/shard_map/dot_general | solution.py:15
  (3 shorter events, 0.0 us)
Async XLA Ops:
  7.2 158.3 %all-reduce.2.cloned.1.call-start = ((), (), s32[]{:S(2)}) async-start(), calls=%async_computation | async-start | bytes 4915200 | tf_op jit(solution)/shard_map/psum | solution.py:145
  27.3 141.1 %copy-start = (f32[2]{0:T(128)S(1)}, f32[2]{0:T(128)}, u32[]{:S(2)}) copy-start(f32[2]{0:T(128)} %constant.20.clone.count_ref) | copy-start | bytes 28
  166.4 51.9 %copy-start.1 = (f32[1536,768]{1,0:T(8,128)S(1)}, f32[1536,768]{1,0:T(8,128)}, u32[]{:S(2)}) copy-start(f32[1536,768]{1,0:T(8,128)} %param.2) | copy-start | bytes 14155780
Sparse Core Ops, SparseCore 0:
  27.5 137.9 all-reduce.1

commit v2 on v1

--- a/solution.py
+++ b/solution.py
@@ -8,6 +8,7 @@
 AXES = ("grp", "wide")
 LANES = 128
 SUB = 8
+TILE = 256
 HIGHEST = lax.Precision.HIGHEST
 
 
@@ -70,13 +71,159 @@
             unit[p] = unit[p] - sum(c * x for c, x in zip(column, carried))
 
 
-def factor_kernel(gram_ref, means_ref, count_ref, factor_ref, inverse_ref, work, upper, inverse):
-    width = gram_ref.shape[0]
+def split(values):
+    high = values.astype(jnp.bfloat16)
+    return high, (values - high.astype(jnp.float32)).astype(jnp.bfloat16)
+
+
+def fast_dot(a, b, dims):
+    return lax.dot_general(a, b, (dims, ((), ())), preferred_element_type=jnp.float32)
+
+
+def upper_blocks(width):
+    n = width // LANES
+    return [(i, j) for i in range(n) for j in range(i, n)]
+
+
+def gram_kernel(x_ref, packed_ref, mean_ref, both_ref, swapped_ref):
+    rows, width = x_ref.shape
+    total = jnp.zeros((SUB, width), jnp.float32)
+    for r in range(0, rows, LANES):
+        part = x_ref[r : r + LANES, :]
+        for q in range(0, LANES, SUB):
+            total = total + part[q : q + SUB, :]
+    mean = jnp.sum(total, axis=0, keepdims=True) * (1.0 / rows)
+    for r in range(0, rows, LANES):
+        high, low = split(x_ref[r : r + LANES, :] - mean)
+        both_ref[r : r + LANES, :] = high
+        both_ref[rows + r : rows + r + LANES, :] = low
+        swapped_ref[r : r + LANES, :] = low
+        swapped_ref[rows + r : rows + r + LANES, :] = high
+    place = {block: LANES * p for p, block in enumerate(upper_blocks(width))}
+    for left in range(0, width, TILE):
+        turned = both_ref[:, left : left + TILE].T
+        for right in range(left, width, TILE):
+            here = slice(right, right + TILE)
+            tile = fast_dot(turned, both_ref[:, here], ((1,), (0,)))
+            tile = tile + fast_dot(turned, swapped_ref[:, here], ((1,), (0,)))
+            for a in range(0, TILE, LANES):
+                for b in range(0, TILE, LANES):
+                    block = ((left + a) // LANES, (right + b) // LANES)
+                    if block in place:
+                        packed_ref[place[block] : place[block] + LANES, :] = tile[
+                            a : a + LANES, b : b + LANES
+                        ]
+    used = LANES * len(place)
+    if packed_ref.shape[0] > used:
+        packed_ref[used:, :] = jnp.zeros((packed_ref.shape[0] - used, LANES), jnp.float32)
+    mean_ref[...] = jnp.zeros(mean_ref.shape, jnp.float32)
+    for b in range(width // LANES):
+        mean_ref[b : b + 1, :] = mean[:, LANES * b : LANES * (b + 1)]
+
+
+def local_gram(embeddings, packed_rows, mean_rows):
+    rows, width = embeddings.shape
+    return pl.pallas_call(
+        gram_kernel,
+        out_shape=(
+            jax.ShapeDtypeStruct((packed_rows, LANES), jnp.float32),
+            jax.ShapeDtypeStruct((mean_rows, LANES), jnp.float32),
+        ),
+        in_specs=[pl.BlockSpec(memory_space=pltpu.VMEM)],
+        out_specs=(pl.BlockSpec(memory_space=pltpu.VMEM),) * 2,
+        scratch_shapes=[pltpu.VMEM((2 * rows, width), jnp.bfloat16)] * 2,
+        compiler_params=pltpu.CompilerParams(vmem_limit_bytes=48 * 2**20),
+    )(embeddings)
+
+
+def exchange_orders(bits):
+    body = [b for b in (3, 1) + tuple(range(4, bits)) if b < bits]
+    tail = [2] if bits > 2 else []
+    return [0] + body + tail, [0] + body[-1:] + body[:-1] + tail
+
+
+def sum_in_pieces(packed, mean_rows):
+    devices = lax.axis_size("grp") * lax.axis_size("wide")
+    bits = devices.bit_length() - 1
+    orders = exchange_orders(bits)
+    me = lax.axis_index(AXES)
+    on_core = me & 1
+
+    def partners(step):
+        return [(d, d ^ (1 << orders[d & 1][step])) for d in range(devices)]
+
+    def bit_at(step, core):
+        return jnp.where(core == 0, me >> orders[0][step], me >> orders[1][step]) & 1
+
+    mine, twin = on_core, 1 - on_core
+    for step in range(1, bits):
+        mine = mine * 2 + bit_at(step, on_core)
+        twin = twin * 2 + bit_at(step, 1 - on_core)
+    piece = packed
+    for step in range(bits):
+        bit = bit_at(step, on_core)
+        half = piece.shape[0] // 2
+        sent = lax.dynamic_slice_in_dim(piece, (1 - bit) * half, half, 0)
+        kept = lax.dynamic_slice_in_dim(piece, bit * half, half, 0)
+        piece = kept + lax.ppermute(sent, AXES, partners(step))
+    held = jnp.concatenate([piece, mean_rows], axis=0)[None]
+    for step in reversed(range(bits)):
+        other = lax.ppermute(held, AXES, partners(step))
+        if step:
+            held = jnp.concatenate([held, other], axis=0)
+    return held, other, jnp.stack([mine, twin])
+
+
+def factor_kernel(
+    held_ref,
+    other_ref,
+    numbers_ref,
+    count_ref,
+    factor_ref,
+    high_ref,
+    low_ref,
+    mean_ref,
+    work,
+    packed,
+    means_scr,
+    upper,
+    inverse,
+):
+    half = held_ref.shape[0]
+    pieces = 2 * half
+    width = factor_ref.shape[0]
     blocks = width // LANES
-    means = means_ref[...]
-    apart = means - jnp.mean(means, axis=0, keepdims=True)
-    between = dot(apart, apart, ((0,), (0,)))
-    work[...] = gram_ref[...] + between * count_ref[0]
+    piece_rows = packed.shape[0] // pieces
+    for part, ref in enumerate((held_ref, other_ref)):
+
+        def unpack(q, _):
+            p = numbers_ref[part] ^ q
+            to = pl.multiple_of(p * piece_rows, SUB)
+            packed[pl.ds(to, piece_rows), :] = ref[q, :piece_rows, :]
+            to = pl.multiple_of(p * SUB, SUB)
+            means_scr[pl.ds(to, SUB), :] = ref[q, piece_rows : piece_rows + SUB, :]
+            return 0
+
+        lax.fori_loop(0, half, unpack, 0, unroll=True)
+
+    stacked = means_scr[...].reshape(pieces, SUB, LANES)
+    middle = jnp.mean(stacked, axis=0)
+    apart = stacked - middle[None]
+    wide = jnp.concatenate([apart[:, b, :] for b in range(blocks)], axis=1)
+    for b in range(blocks):
+        mean_ref[:, LANES * b : LANES * (b + 1)] = jnp.broadcast_to(
+            middle[b : b + 1, :], (SUB, LANES)
+        )
+    at = 0
+    for i in range(blocks):
+        rows = slice(LANES * i, LANES * (i + 1))
+        between = dot(wide[:, rows], wide[:, LANES * i :], ((0,), (0,))) * count_ref[0]
+        for j in range(i, blocks):
+            work[rows, LANES * j : LANES * (j + 1)] = (
+                packed[at : at + LANES, :]
+                + between[:, LANES * (j - i) : LANES * (j - i + 1)]
+            )
+            at += LANES
     total_scale = count_ref[1]
     row_at = lax.broadcasted_iota(jnp.int32, (LANES, width), 0)
     col_at = lax.broadcasted_iota(jnp.int32, (LANES, width), 1)
@@ -92,9 +239,11 @@
             col_at >= row_at + start, work[here, :] * (1.0 / total_scale), 0.0
         )
         work[here, here] = inverse[...]
-        inverse_ref[here, :] = jnp.where(
-            col_at <= row_at + start, work[here, :] * total_scale, 0.0
+        high, low = split(
+            jnp.where(col_at <= row_at + start, work[here, :] * total_scale, 0.0)
         )
+        high_ref[here, :] = high
+        low_ref[here, :] = low
 
         def below(i, _):
             there = pl.ds(pl.multiple_of(i * LANES, LANES), LANES)
@@ -110,44 +259,73 @@
     lax.fori_loop(0, blocks, stage, 0)
 
 
-def factor_and_inverse(gram, means, local_rows, row_count):
-    width = gram.shape[0]
-    square = jax.ShapeDtypeStruct((width, width), jnp.float32)
-    counts = jnp.array([local_rows, row_count**0.5], jnp.float32)
+def factor_and_inverse(held, other, numbers, piece_rows, width, local_rows):
+    pieces = 2 * held.shape[0]
+    vmem = pl.BlockSpec(memory_space=pltpu.VMEM)
+    smem = pl.BlockSpec(memory_space=pltpu.SMEM)
+    half_type = jax.ShapeDtypeStruct((width, width), jnp.bfloat16)
+    counts = jnp.array([local_rows, (local_rows * pieces) ** 0.5], jnp.float32)
     return pl.pallas_call(
         factor_kernel,
-        out_shape=(square, square),
-        in_specs=[
-            pl.BlockSpec(memory_space=pltpu.VMEM),
-            pl.BlockSpec(memory_space=pltpu.VMEM),
-            pl.BlockSpec(memory_space=pltpu.SMEM),
-        ],
-        out_specs=(pl.BlockSpec(memory_space=pltpu.VMEM),) * 2,
+        out_shape=(
+            jax.ShapeDtypeStruct((width, width), jnp.float32),
+            half_type,
+            half_type,
+            jax.ShapeDtypeStruct((SUB, width), jnp.float32),
+        ),
+        in_specs=[vmem, vmem, smem, smem],
+        out_specs=(vmem,) * 4,
         scratch_shapes=[
             pltpu.VMEM((width, width), jnp.float32),
+            pltpu.VMEM((pieces * piece_rows, LANES), jnp.float32),
+            pltpu.VMEM((pieces * SUB, LANES), jnp.float32),
             pltpu.VMEM((LANES, LANES), jnp.float32),
             pltpu.VMEM((LANES, LANES), jnp.float32),
         ],
-        compiler_params=pltpu.CompilerParams(vmem_limit_bytes=40 * 2**20),
-    )(gram, means, counts)
+        compiler_params=pltpu.CompilerParams(vmem_limit_bytes=48 * 2**20),
+    )(held, other, numbers, counts)
+
+
+def whiten_kernel(x_ref, mean_ref, high_ref, low_ref, out_ref):
+    width = x_ref.shape[1]
+    high, low = split(x_ref[...] - mean_ref[:1, :])
+    for right in range(0, width, TILE):
+        here = slice(right, right + TILE)
+        deep = slice(0, right + TILE)
+        tile = fast_dot(high[:, deep], high_ref[here, deep], ((1,), (1,)))
+        tile = tile + fast_dot(high[:, deep], low_ref[here, deep], ((1,), (1,)))
+        out_ref[:, here] = tile + fast_dot(low[:, deep], high_ref[here, deep], ((1,), (1,)))
+
+
+def whiten(embeddings, mean, high, low):
+    rows, width = embeddings.shape
+    whole = lambda i: (0, 0)
+    return pl.pallas_call(
+        whiten_kernel,
+        grid=(rows // TILE,),
+        out_shape=jax.ShapeDtypeStruct((rows, width), jnp.float32),
+        in_specs=[
+            pl.BlockSpec((TILE, width), lambda i: (i, 0)),
+            pl.BlockSpec(mean.shape, whole),
+            pl.BlockSpec((width, width), whole),
+            pl.BlockSpec((width, width), whole),
+        ],
+        out_specs=pl.BlockSpec((TILE, width), lambda i: (i, 0)),
+        compiler_params=pltpu.CompilerParams(vmem_limit_bytes=48 * 2**20),
+    )(embeddings, mean, high, low)
 
 
 def shards(embeddings):
     local_rows, width = embeddings.shape
     devices = lax.axis_size("grp") * lax.axis_size("wide")
-    row_count = local_rows * devices
-    me = lax.axis_index(AXES)
-    mean = jnp.sum(embeddings, axis=0, keepdims=True) / local_rows
-    centred = embeddings - mean
-    gram = dot(centred, centred, ((0,), (0,)))
-    mine = lax.broadcasted_iota(jnp.int32, (devices, 1), 0) == me
-    payload = jnp.concatenate([gram, jnp.where(mine, mean, 0.0)], axis=0)
-    payload = lax.psum(payload, AXES)
-    means = payload[width:]
-    factor, inverse = factor_and_inverse(payload[:width], means, local_rows, row_count)
-    col_mean = jnp.mean(means, axis=0, keepdims=True)
-    whitened = dot(embeddings - col_mean, inverse, ((1,), (1,)))
-    return (whitened, factor)
+    used = LANES * len(upper_blocks(width))
+    piece_rows = -(-used // (SUB * devices)) * SUB
+    packed, mean_rows = local_gram(embeddings, piece_rows * devices, SUB)
+    held, other, numbers = sum_in_pieces(packed, mean_rows)
+    factor, high, low, mean = factor_and_inverse(
+        held, other, numbers, piece_rows, width, local_rows
+    )
+    return (whiten(embeddings, mean, high, low), factor)
 
 
 def solution(mesh):

time: 238 us -> 120 us (0.50)
  waiting for transfers between devices: 138 us -> 32.2 us
  matrix products: 28.8 us -> 0 us
  starting transfers between devices: 0.04 us -> 20.7 us
  Pallas kernels: 49.9 us -> 63.6 us
  between operations: 14.1 us -> 0.81 us
  other arithmetic: 5.29 us -> 0.32 us
    psum x1 -> x0, waiting for transfers between devices: 138 us -> none  [shards(): payload = lax.psum(payload, AXES)]
    ppermute x0 -> x10, waiting for transfers between devices: none -> 32.2 us  [the longest x5 16.9 us: sum_in_pieces(): other = lax.ppermute(held, AXES, partners(step))]
    dot_general x2 -> x0, matrix products: 28.8 us -> none  [dot(): lax.dot_general(a, b, (dims, ((), ())), precision=HIGHEST, preferred_elem...]
    ppermute x0 -> x10, starting transfers between devices: none -> 20.7 us  [the longest x5 10.7 us: sum_in_pieces(): piece = kept + lax.ppermute(sent, AXES, partners(step))]
    pallas_call x1 -> x3, Pallas kernels: 49.9 us -> 63.6 us  [the longest x1 49.9 us: factor_and_inverse(): pl.pallas_call(factor_kernel, out_shape=(jax.ShapeDtypeStruct((width, wid...]
    reduce_sum x2 -> x0, other arithmetic: 3.6 us -> none  [the longest x1 2.69 us: shards(): mean = jnp.sum(embeddings, axis=0, keepdims=True) / local_rows]
  transfers between devices with their start and end apart: 1 -> 10, of which waited for: 1 -> 10; matrix products, arithmetic and copies ran while one was open for 0% -> 0% of each run, Pallas kernels for 0% -> 0%
where the time goes in v2:
time: 120 us
  Pallas kernels  63.6 us (53%)
  waiting for transfers between devices  32.2 us (27%)
  starting transfers between devices  20.7 us (17%)
  local copies, waits for them, and re-layouts  2.54 us (2%)
    pallas_call x1, Pallas kernels, factor_and_inverse(): pl.pallas_call(factor_kernel, out_shape=(jax.ShapeDtypeStruct((width, wid...  49.9 us
    ppermute x5, waiting for transfers between devices, sum_in_pieces(): other = lax.ppermute(held, AXES, partners(step))  16.9 us
    ppermute x5, waiting for transfers between devices, sum_in_pieces(): piece = kept + lax.ppermute(sent, AXES, partners(step))  15.3 us
    ppermute x5, starting transfers between devices, sum_in_pieces(): piece = kept + lax.ppermute(sent, AXES, partners(step))  10.7 us
    ppermute x5, starting transfers between devices, sum_in_pieces(): other = lax.ppermute(held, AXES, partners(step))  9.92 us
    pallas_call x1, Pallas kernels, whiten(): pl.pallas_call(whiten_kernel, grid=(rows // TILE,), out_shape=jax.ShapeDt...  8.29 us
    pallas_call x1, Pallas kernels, local_gram(): pl.pallas_call(gram_kernel, out_shape=(jax.ShapeDtypeStruct((packed_rows,...  5.41 us
  transfers between devices with their start and end apart: 10, of which 10 were waited for; matrix products, arithmetic and copies ran while one was open for 0% of the time, Pallas kernels for 0%

profile of v2, /device:TPU:0, one launch (start us, length us, event | category | flops | bytes accessed | tf_op | source)
XLA Modules:
  0.0 120.1 jit_solution(3656116368353490618)
XLA Ops:
  0.6 0.0 copy-start
  0.6 2.3 %copy-done = f32[1536,768]{1,0:T(8,128)S(1)} copy-done((f32[1536,768]{1,0:T(8,128)S(1)}, f32[1536,768]{1,0:T(8,128)}, u32[]{:S(2)}) %copy-start) | copy-done | bytes 4718616
  3.0 5.4 %shard_map.41 = (f32[2816,128]{1,0:T(8,128)S(1)}, f32[8,128]{1,0:T(8,128)S(1)}) custom-call(f32[1536,768]{1,0:T(8,128)S(1)} %copy-done), custom_call_target="tpu_custom_call" | custom-call | tf_op jit(solution)/shard_map/pallas_call | solution.py:126
  8.4 0.1 constant_dynamic-slice_fusion.4
  8.5 0.5 collective-permute-start
  9.0 1.8 %collective-permute-done = f32[1408,128]{1,0:T(8,128)S(1)} collective-permute-done((f32[1408,128]{1,0:T(8,128)S(1)}, f32[1408,128]{1,0:T(8,128)S(1)}, u32[]{:S(2)}, u32[]{:S(2)}) %collective-permute-start) | collective-permute-done | bytes 720928 | tf_op jit(solution)/shard_map/ppermute | solution.py:168
  10.8 0.1 dynamic-slice_add_fusion
  10.9 2.9 %collective-permute-start.1 = (f32[704,128]{1,0:T(8,128)S(1)}, f32[704,128]{1,0:T(8,128)S(1)}, u32[]{:S(2)}, u32[]{:S(2)}) collective-permute-start(f32[704,128]{1,0:T(8,128)S(1)} %constant_dynamic-slice_fusion.3), channel_id=1, source_target_pairs={{0,8},{1,17},{2,10},{3,19},{4,12},{5,21},{6,14},{7,23},{8,0},{9,25... | collective-permute-start | bytes 1081352 | tf_op jit(solution)/shard_map/ppermute | solution.py:168
  13.9 5.4 %collective-permute-done.1 = f32[704,128]{1,0:T(8,128)S(1)} collective-permute-done((f32[704,128]{1,0:T(8,128)S(1)}, f32[704,128]{1,0:T(8,128)S(1)}, u32[]{:S(2)}, u32[]{:S(2)}) %collective-permute-start.1) | collective-permute-done | bytes 360480 | tf_op jit(solution)/shard_map/ppermute | solution.py:168
  19.3 2.2 %collective-permute-start.2 = (f32[352,128]{1,0:T(8,128)S(1)}, f32[352,128]{1,0:T(8,128)S(1)}, u32[]{:S(2)}, u32[]{:S(2)}) collective-permute-start(f32[352,128]{1,0:T(8,128)S(1)} %constant_dynamic-slice_fusion.2), channel_id=1, source_target_pairs={{0,2},{1,9},{2,0},{3,11},{4,6},{5,13},{6,4},{7,15},{8,10},{9,1},{1... | collective-permute-start | bytes 540680 | tf_op jit(solution)/shard_map/ppermute | solution.py:168
  21.5 3.5 %collective-permute-done.2 = f32[352,128]{1,0:T(8,128)S(1)} collective-permute-done((f32[352,128]{1,0:T(8,128)S(1)}, f32[352,128]{1,0:T(8,128)S(1)}, u32[]{:S(2)}, u32[]{:S(2)}) %collective-permute-start.2) | collective-permute-done | bytes 180256 | tf_op jit(solution)/shard_map/ppermute | solution.py:168
  25.0 2.0 %collective-permute-start.3 = (f32[176,128]{1,0:T(8,128)S(1)}, f32[176,128]{1,0:T(8,128)S(1)}, u32[]{:S(2)}, u32[]{:S(2)}) collective-permute-start(f32[176,128]{1,0:T(8,128)S(1)} %constant_dynamic-slice_fusion.1), channel_id=1, source_target_pairs={{0,16},{1,3},{2,18},{3,1},{4,20},{5,7},{6,22},{7,5},{8,24},{9,11},... | collective-permute-start | bytes 270344 | tf_op jit(solution)/shard_map/ppermute | solution.py:168
  27.1 2.6 %collective-permute-done.3 = f32[176,128]{1,0:T(8,128)S(1)} collective-permute-done((f32[176,128]{1,0:T(8,128)S(1)}, f32[176,128]{1,0:T(8,128)S(1)}, u32[]{:S(2)}, u32[]{:S(2)}) %collective-permute-start.3) | collective-permute-done | bytes 90144 | tf_op jit(solution)/shard_map/ppermute | solution.py:168
  29.7 3.1 %collective-permute-start.4 = (f32[88,128]{1,0:T(8,128)S(1)}, f32[88,128]{1,0:T(8,128)S(1)}, u32[]{:S(2)}, u32[]{:S(2)}) collective-permute-start(f32[88,128]{1,0:T(8,128)S(1)} %constant_dynamic-slice_fusion), channel_id=1, source_target_pairs={{0,4},{1,5},{2,6},{3,7},{4,0},{5,1},{6,2},{7,3},{8,12},{9,13},{10,... | collective-permute-start | bytes 135176 | tf_op jit(solution)/shard_map/ppermute | solution.py:168
  32.8 2.0 %collective-permute-done.4 = f32[88,128]{1,0:T(8,128)S(1)} collective-permute-done((f32[88,128]{1,0:T(8,128)S(1)}, f32[88,128]{1,0:T(8,128)S(1)}, u32[]{:S(2)}, u32[]{:S(2)}) %collective-permute-start.4) | collective-permute-done | bytes 45088 | tf_op jit(solution)/shard_map/ppermute | solution.py:168
  34.8 3.3 %collective-permute-start.5 = (f32[1,96,128]{2,1,0:T(8,128)S(1)}, f32[1,96,128]{2,1,0:T(8,128)S(1)}, u32[]{:S(2)}, u32[]{:S(2)}) collective-permute-start(f32[1,96,128]{2,1,0:T(8,128)S(1)} %maximum_bitcast_fusion), channel_id=1, source_target_pairs={{0,4},{1,5},{2,6},{3,7},{4,0},{5,1},{6,2},{7,3},{8,12},{9,13},{10,... | collective-permute-start | bytes 147464 | tf_op jit(solution)/shard_map/ppermute | solution.py:171
  38.1 2.1 %collective-permute-done.5 = f32[1,96,128]{2,1,0:T(8,128)S(1)} collective-permute-done((f32[1,96,128]{2,1,0:T(8,128)S(1)}, f32[1,96,128]{2,1,0:T(8,128)S(1)}, u32[]{:S(2)}, u32[]{:S(2)}) %collective-permute-start.5) | collective-permute-done | bytes 49184 | tf_op jit(solution)/shard_map/ppermute | solution.py:171
  40.2 0.0 copy-start.1
  40.2 1.9 %collective-permute-start.6 = (f32[2,96,128]{2,1,0:T(8,128)S(1)}, f32[2,96,128]{2,1,0:T(8,128)S(1)}, u32[]{:S(2)}, u32[]{:S(2)}) collective-permute-start(f32[2,96,128]{2,1,0:T(8,128)S(1)} %pad_maximum_fusion.2), channel_id=1, source_target_pairs={{0,16},{1,3},{2,18},{3,1},{4,20},{5,7},{6,22},{7,5},{8,24},{9,11},... | collective-permute-start | bytes 294920 | tf_op jit(solution)/shard_map/ppermute | solution.py:171
  42.1 2.8 %collective-permute-done.6 = f32[2,96,128]{2,1,0:T(8,128)S(1)} collective-permute-done((f32[2,96,128]{2,1,0:T(8,128)S(1)}, f32[2,96,128]{2,1,0:T(8,128)S(1)}, u32[]{:S(2)}, u32[]{:S(2)}) %collective-permute-start.6) | collective-permute-done | bytes 98336 | tf_op jit(solution)/shard_map/ppermute | solution.py:171
  44.9 3.1 %collective-permute-start.7 = (f32[4,96,128]{2,1,0:T(8,128)S(1)}, f32[4,96,128]{2,1,0:T(8,128)S(1)}, u32[]{:S(2)}, u32[]{:S(2)}) collective-permute-start(f32[4,96,128]{2,1,0:T(8,128)S(1)} %pad_maximum_fusion.1), channel_id=1, source_target_pairs={{0,2},{1,9},{2,0},{3,11},{4,6},{5,13},{6,4},{7,15},{8,10},{9,1},{1... | collective-permute-start | bytes 589832 | tf_op jit(solution)/shard_map/ppermute | solution.py:171
  48.0 3.6 %collective-permute-done.7 = f32[4,96,128]{2,1,0:T(8,128)S(1)} collective-permute-done((f32[4,96,128]{2,1,0:T(8,128)S(1)}, f32[4,96,128]{2,1,0:T(8,128)S(1)}, u32[]{:S(2)}, u32[]{:S(2)}) %collective-permute-start.7) | collective-permute-done | bytes 196640 | tf_op jit(solution)/shard_map/ppermute | solution.py:171
  51.7 1.6 %collective-permute-start.8 = (f32[8,96,128]{2,1,0:T(8,128)S(1)}, f32[8,96,128]{2,1,0:T(8,128)S(1)}, u32[]{:S(2)}, u32[]{:S(2)}) collective-permute-start(f32[8,96,128]{2,1,0:T(8,128)S(1)} %pad_maximum_fusion), channel_id=1, source_target_pairs={{0,8},{1,17},{2,10},{3,19},{4,12},{5,21},{6,14},{7,23},{8,0},{9,25... | collective-permute-start | bytes 1179656 | tf_op jit(solution)/shard_map/ppermute | solution.py:171
  53.3 6.2 %collective-permute-done.8 = f32[8,96,128]{2,1,0:T(8,128)S(1)} collective-permute-done((f32[8,96,128]{2,1,0:T(8,128)S(1)}, f32[8,96,128]{2,1,0:T(8,128)S(1)}, u32[]{:S(2)}, u32[]{:S(2)}) %collective-permute-start.8) | collective-permute-done | bytes 393248 | tf_op jit(solution)/shard_map/ppermute | solution.py:171
  59.6 0.1 collective-permute-start.9
  59.7 0.1 pad_add_fusion.numbers_ref
  59.8 2.2 %collective-permute-done.9.other_ref = f32[16,96,128]{2,1,0:T(8,128)S(1)} collective-permute-done((f32[16,96,128]{2,1,0:T(8,128)S(1)}, f32[16,96,128]{2,1,0:T(8,128)S(1)}, u32[]{:S(2)}, u32[]{:S(2)}) %collective-permute-start.9) | collective-permute-done | bytes 786464 | tf_op jit(solution)/shard_map/ppermute | solution.py:171
  61.9 0.0 copy-done.1
  61.9 49.9 %shard_map.42 = (f32[768,768]{1,0:T(8,128)}, bf16[768,768]{1,0:T(8,128)(2,1)S(1)}, bf16[768,768]{1,0:T(8,128)(2,1)S(1)}, f32[8,768]{1,0:T(8,128)S(1)}) custom-call(f32[16,96,128]{2,1,0:T(8,128)S(1)} %constant_dynamic-update-slice_fusion.held_ref, f32[16,96,128]{2,1,0:T(8,128)S(1)} %collective-permute-done.9.other_ref, s32[2]{0:T(128)S(1)} %pad_add_fusion.numbers_ref, ...), custom_call_target="tpu_custom_call" | custom-call | tf_op jit(solution)/shard_map/pallas_call | solution.py:268
  111.8 8.3 %shard_map.43 = f32[1536,768]{1,0:T(8,128)} custom-call(f32[1536,768]{1,0:T(8,128)} %x_ref.3, f32[8,768]{1,0:T(8,128)S(1)} %get-tuple-element.10.mean_ref, bf16[768,768]{1,0:T(8,128)(2,1)S(1)} %get-tuple-element.11.high_ref, bf16[768,768]{1,0:T(8,128)(2,1)S(1)} %get-tuple-element.12.low_ref), custom_call_target="tpu_custom_call" | custom-call | tf_op jit(solution)/shard_map/pallas_call | solution.py:303
  (17 shorter events, 0.3 us)
Async XLA Ops:
  0.6 2.3 %copy-start = (f32[1536,768]{1,0:T(8,128)S(1)}, f32[1536,768]{1,0:T(8,128)}, u32[]{:S(2)}) copy-start(f32[1536,768]{1,0:T(8,128)} %x_ref.3) | copy-start | bytes 14155780
  8.5 2.3 %collective-permute-start = (f32[1408,128]{1,0:T(8,128)S(1)}, f32[1408,128]{1,0:T(8,128)S(1)}, u32[]{:S(2)}, u32[]{:S(2)}) collective-permute-start(f32[1408,128]{1,0:T(8,128)S(1)} %constant_dynamic-slice_fusion.4), channel_id=1, source_target_pairs={{0,1},{1,0},{2,3},{3,2},{4,5},{5,4},{6,7},{7,6},{8,9},{9,8},{10,11... | collective-permute-start | bytes 2162696 | tf_op jit(solution)/shard_map/ppermute | solution.py:168
  10.9 8.3 %collective-permute-start.1 = (f32[704,128]{1,0:T(8,128)S(1)}, f32[704,128]{1,0:T(8,128)S(1)}, u32[]{:S(2)}, u32[]{:S(2)}) collective-permute-start(f32[704,128]{1,0:T(8,128)S(1)} %constant_dynamic-slice_fusion.3), channel_id=1, source_target_pairs={{0,8},{1,17},{2,10},{3,19},{4,12},{5,21},{6,14},{7,23},{8,0},{9,25... | collective-permute-start | bytes 1081352 | tf_op jit(solution)/shard_map/ppermute | solution.py:168
  19.3 5.6 %collective-permute-start.2 = (f32[352,128]{1,0:T(8,128)S(1)}, f32[352,128]{1,0:T(8,128)S(1)}, u32[]{:S(2)}, u32[]{:S(2)}) collective-permute-start(f32[352,128]{1,0:T(8,128)S(1)} %constant_dynamic-slice_fusion.2), channel_id=1, source_target_pairs={{0,2},{1,9},{2,0},{3,11},{4,6},{5,13},{6,4},{7,15},{8,10},{9,1},{1... | collective-permute-start | bytes 540680 | tf_op jit(solution)/shard_map/ppermute | solution.py:168
  25.0 4.6 %collective-permute-start.3 = (f32[176,128]{1,0:T(8,128)S(1)}, f32[176,128]{1,0:T(8,128)S(1)}, u32[]{:S(2)}, u32[]{:S(2)}) collective-permute-start(f32[176,128]{1,0:T(8,128)S(1)} %constant_dynamic-slice_fusion.1), channel_id=1, source_target_pairs={{0,16},{1,3},{2,18},{3,1},{4,20},{5,7},{6,22},{7,5},{8,24},{9,11},... | collective-permute-start | bytes 270344 | tf_op jit(solution)/shard_map/ppermute | solution.py:168
  29.7 5.1 %collective-permute-start.4 = (f32[88,128]{1,0:T(8,128)S(1)}, f32[88,128]{1,0:T(8,128)S(1)}, u32[]{:S(2)}, u32[]{:S(2)}) collective-permute-start(f32[88,128]{1,0:T(8,128)S(1)} %constant_dynamic-slice_fusion), channel_id=1, source_target_pairs={{0,4},{1,5},{2,6},{3,7},{4,0},{5,1},{6,2},{7,3},{8,12},{9,13},{10,... | collective-permute-start | bytes 135176 | tf_op jit(solution)/shard_map/ppermute | solution.py:168
  34.8 5.4 %collective-permute-start.5 = (f32[1,96,128]{2,1,0:T(8,128)S(1)}, f32[1,96,128]{2,1,0:T(8,128)S(1)}, u32[]{:S(2)}, u32[]{:S(2)}) collective-permute-start(f32[1,96,128]{2,1,0:T(8,128)S(1)} %maximum_bitcast_fusion), channel_id=1, source_target_pairs={{0,4},{1,5},{2,6},{3,7},{4,0},{5,1},{6,2},{7,3},{8,12},{9,13},{10,... | collective-permute-start | bytes 147464 | tf_op jit(solution)/shard_map/ppermute | solution.py:171
  40.2 21.7 %copy-start.1 = (f32[2]{0:T(128)S(1)}, f32[2]{0:T(128)}, u32[]{:S(2)}) copy-start(f32[2]{0:T(128)} %constant.34.clone.count_ref) | copy-start | bytes 28
  40.2 4.7 %collective-permute-start.6 = (f32[2,96,128]{2,1,0:T(8,128)S(1)}, f32[2,96,128]{2,1,0:T(8,128)S(1)}, u32[]{:S(2)}, u32[]{:S(2)}) collective-permute-start(f32[2,96,128]{2,1,0:T(8,128)S(1)} %pad_maximum_fusion.2), channel_id=1, source_target_pairs={{0,16},{1,3},{2,18},{3,1},{4,20},{5,7},{6,22},{7,5},{8,24},{9,11},... | collective-permute-start | bytes 294920 | tf_op jit(solution)/shard_map/ppermute | solution.py:171
  44.9 6.8 %collective-permute-start.7 = (f32[4,96,128]{2,1,0:T(8,128)S(1)}, f32[4,96,128]{2,1,0:T(8,128)S(1)}, u32[]{:S(2)}, u32[]{:S(2)}) collective-permute-start(f32[4,96,128]{2,1,0:T(8,128)S(1)} %pad_maximum_fusion.1), channel_id=1, source_target_pairs={{0,2},{1,9},{2,0},{3,11},{4,6},{5,13},{6,4},{7,15},{8,10},{9,1},{1... | collective-permute-start | bytes 589832 | tf_op jit(solution)/shard_map/ppermute | solution.py:171
  51.7 7.8 %collective-permute-start.8 = (f32[8,96,128]{2,1,0:T(8,128)S(1)}, f32[8,96,128]{2,1,0:T(8,128)S(1)}, u32[]{:S(2)}, u32[]{:S(2)}) collective-permute-start(f32[8,96,128]{2,1,0:T(8,128)S(1)} %pad_maximum_fusion), channel_id=1, source_target_pairs={{0,8},{1,17},{2,10},{3,19},{4,12},{5,21},{6,14},{7,23},{8,0},{9,25... | collective-permute-start | bytes 1179656 | tf_op jit(solution)/shard_map/ppermute | solution.py:171
  59.6 2.4 %collective-permute-start.9 = (f32[16,96,128]{2,1,0:T(8,128)S(1)}, f32[16,96,128]{2,1,0:T(8,128)S(1)}, u32[]{:S(2)}, u32[]{:S(2)}) collective-permute-start(f32[16,96,128]{2,1,0:T(8,128)S(1)} %constant_dynamic-update-slice_fusion.held_ref), channel_id=1, source_target_pairs={{0,1},{1,0},{2,3},{3,2},{4,5},{5,4},{6,7},{7,6},{8,9},{9,8},{10,11... | collective-permute-start | bytes 2359304 | tf_op jit(solution)/shard_map/ppermute | solution.py:171

commit v3 on v2

--- a/solution.py
+++ b/solution.py
@@ -24,51 +24,6 @@
 
 def over_rows(tile, row):
     return jnp.broadcast_to(tile[row : row + 1, :], (SUB, LANES))
-
-
-def factor_block(block, upper_ref, inverse_ref):
-    groups = LANES // SUB
-    tiles = [block[SUB * p : SUB * (p + 1), :] for p in range(groups)]
-    row_at = lax.broadcasted_iota(jnp.int32, (SUB, LANES), 0)
-    lane_at = lax.broadcasted_iota(jnp.int32, (SUB, LANES), 1)
-    unit = [
-        jnp.where(lane_at == row_at + SUB * p, 1.0, 0.0).astype(jnp.float32)
-        for p in range(groups)
-    ]
-    for g in range(groups):
-        base = SUB * g
-        rows = [over_rows(tiles[g], i) for i in range(SUB)]
-        carried = [over_rows(unit[g], i) for i in range(SUB)]
-        s = {
-            (i, j): over_lanes(rows[i], base + j) for i in range(SUB) for j in range(i, SUB)
-        }
-        scale = []
-        for j in range(SUB):
-            r = lax.rsqrt(s[j, j])
-            scale.append(r)
-            rows[j] = rows[j] * r
-            carried[j] = carried[j] * r
-            for k in range(j + 1, SUB):
-                s[j, k] = s[j, k] * r
-            for k in range(j + 1, SUB):
-                for m in range(k, SUB):
-                    s[k, m] = s[k, m] - s[j, k] * s[j, m]
-                rows[k] = rows[k] - s[j, k] * rows[j]
-                carried[k] = carried[k] - s[j, k] * carried[j]
-            upper_ref[base + j : base + j + 1, :] = rows[j][:1, :]
-            inverse_ref[base + j : base + j + 1, :] = carried[j][:1, :]
-        if g == groups - 1:
-            break
-        for i in reversed(range(SUB)):
-            for k in range(i + 1, SUB):
-                rows[i] = rows[i] - s[i, k] * rows[k]
-                carried[i] = carried[i] - s[i, k] * carried[k]
-            rows[i] = rows[i] * scale[i]
-            carried[i] = carried[i] * scale[i]
-        for p in range(g + 1, groups):
-            column = [over_lanes(tiles[p], base + i) for i in range(SUB)]
-            tiles[p] = tiles[p] - sum(c * x for c, x in zip(column, rows))
-            unit[p] = unit[p] - sum(c * x for c, x in zip(column, carried))
 
 
 def split(values):
@@ -174,6 +129,90 @@
     return held, other, jnp.stack([mine, twin])
 
 
+def factor_block(block, upper_ref, inverse_ref):
+    groups = LANES // SUB
+    tiles = [block[SUB * p : SUB * (p + 1), :] for p in range(groups)]
+    row_at = lax.broadcasted_iota(jnp.int32, (SUB, LANES), 0)
+    lane_at = lax.broadcasted_iota(jnp.int32, (SUB, LANES), 1)
+    unit = [
+        jnp.where(lane_at == row_at + SUB * p, 1.0, 0.0).astype(jnp.float32)
+        for p in range(groups)
+    ]
+    for g in range(groups):
+        base = SUB * g
+        ahead = g + 1 < groups
+        rows = [over_rows(tiles[g], i) for i in range(SUB)]
+        s = {
+            (i, j): over_lanes(rows[i], base + j) for i in range(SUB) for j in range(i, SUB)
+        }
+        carried = [over_rows(unit[g], i) for i in range(SUB)]
+        if ahead:
+            column = [over_lanes(tiles[g + 1], base + i) for i in range(SUB)]
+        scale = []
+        for j in range(SUB):
+            r = lax.rsqrt(s[j, j])
+            scale.append(r)
+            for k in range(j + 1, SUB):
+                s[j, k] = s[j, k] * r
+            for k in range(j + 1, SUB):
+                for m in range(k, SUB):
+                    s[k, m] = s[k, m] - s[j, k] * s[j, m]
+            rows[j] = rows[j] * r
+            carried[j] = carried[j] * r
+            for k in range(j + 1, SUB):
+                rows[k] = rows[k] - s[j, k] * rows[j]
+                carried[k] = carried[k] - s[j, k] * carried[j]
+            if ahead:
+                column[j] = column[j] * r
+                for k in range(j + 1, SUB):
+                    column[k] = column[k] - column[j] * s[j, k]
+                tiles[g + 1] = tiles[g + 1] - column[j] * rows[j]
+                unit[g + 1] = unit[g + 1] - column[j] * carried[j]
+            upper_ref[base + j : base + j + 1, :] = rows[j][:1, :]
+            inverse_ref[base + j : base + j + 1, :] = carried[j][:1, :]
+        if g + 2 < groups:
+            for i in reversed(range(SUB)):
+                for k in range(i + 1, SUB):
+                    rows[i] = rows[i] - s[i, k] * rows[k]
+                    carried[i] = carried[i] - s[i, k] * carried[k]
+                rows[i] = rows[i] * scale[i]
+                carried[i] = carried[i] * scale[i]
+        for p in range(g + 2, groups):
+            column = [over_lanes(tiles[p], base + i) for i in range(SUB)]
+            tiles[p] = tiles[p] - tree_sum([c * x for c, x in zip(column, rows)])
+            unit[p] = unit[p] - tree_sum([c * x for c, x in zip(column, carried)])
+        yield
+
+
+def tree_sum(terms):
+    while len(terms) > 1:
+        terms = [a + b for a, b in zip(terms[::2], terms[1::2])]
+    return terms[0]
+
+
+def in_three(values):
+    high = values.astype(jnp.bfloat16)
+    rest = values - high.astype(jnp.float32)
+    middle = rest.astype(jnp.bfloat16)
+    return high, middle, (rest - middle.astype(jnp.float32)).astype(jnp.bfloat16)
+
+
+def left_parts(values):
+    high, middle, low = in_three(values)
+    return jnp.concatenate([high, middle], axis=1), jnp.concatenate([low, high], axis=1)
+
+
+def right_parts(values):
+    high, middle, low = in_three(values)
+    stack = lambda a, b: jnp.concatenate([a, b], axis=0)
+    return stack(high, high), stack(middle, middle), stack(high, low)
+
+
+def parts_dot(left, right):
+    plain = lambda a, b: fast_dot(a, b, ((1,), (0,)))
+    return (plain(left[1], right[2]) + plain(left[0], right[1])) + plain(left[0], right[0])
+
+
 def factor_kernel(
     held_ref,
     other_ref,
@@ -186,14 +225,15 @@
     work,
     packed,
     means_scr,
-    upper,
-    inverse,
+    upper_ref,
+    inverse_ref,
 ):
     half = held_ref.shape[0]
     pieces = 2 * half
     width = factor_ref.shape[0]
     blocks = width // LANES
     piece_rows = packed.shape[0] // pieces
+
     for part, ref in enumerate((held_ref, other_ref)):
 
         def unpack(q, _):
@@ -214,49 +254,102 @@
         mean_ref[:, LANES * b : LANES * (b + 1)] = jnp.broadcast_to(
             middle[b : b + 1, :], (SUB, LANES)
         )
-    at = 0
-    for i in range(blocks):
-        rows = slice(LANES * i, LANES * (i + 1))
-        between = dot(wide[:, rows], wide[:, LANES * i :], ((0,), (0,))) * count_ref[0]
-        for j in range(i, blocks):
-            work[rows, LANES * j : LANES * (j + 1)] = (
-                packed[at : at + LANES, :]
-                + between[:, LANES * (j - i) : LANES * (j - i + 1)]
+    total_scale = count_ref[1]
+    place = {block: LANES * p for p, block in enumerate(upper_blocks(width))}
+    span = lambda b, e=None: slice(LANES * b, LANES * (b + 1 if e is None else e))
+
+    def gather(i, first, end):
+        between = dot(wide[:, span(i)], wide[:, span(first, end)], ((0,), (0,)))
+        for j in range(first, end):
+            work[span(i), span(j)] = (
+                packed[place[i, j] : place[i, j] + LANES, :]
+                + between[:, span(j - first)] * count_ref[0]
             )
-            at += LANES
-    total_scale = count_ref[1]
-    row_at = lax.broadcasted_iota(jnp.int32, (LANES, width), 0)
-    col_at = lax.broadcasted_iota(jnp.int32, (LANES, width), 1)
-
-    def stage(k, _):
-        start = pl.multiple_of(k * LANES, LANES)
-        here = pl.ds(start, LANES)
-        factor_block(work[here, here], upper, inverse)
-        solved = dot(inverse[...], work[here, :], ((1,), (0,)))
-        work[here, :] = solved
-        work[here, here] = upper[...]
-        factor_ref[here, :] = jnp.where(
-            col_at >= row_at + start, work[here, :] * (1.0 / total_scale), 0.0
-        )
-        work[here, here] = inverse[...]
-        high, low = split(
-            jnp.where(col_at <= row_at + start, work[here, :] * total_scale, 0.0)
-        )
-        high_ref[here, :] = high
-        low_ref[here, :] = low
-
-        def below(i, _):
-            there = pl.ds(pl.multiple_of(i * LANES, LANES), LANES)
-            work[there, here] = jnp.zeros((LANES, LANES), jnp.float32)
-            work[there, :] = work[there, :] - dot(
-                work[here, there], work[here, :], ((0,), (0,))
+
+    def write_row(k):
+        row_at = lax.broadcasted_iota(jnp.int32, (LANES, LANES), 0)
+        col_at = lax.broadcasted_iota(jnp.int32, (LANES, LANES), 1)
+        zero = jnp.zeros((LANES, LANES), jnp.float32)
+        for j in range(blocks):
+            if j < k:
+                factor, back = zero, work[span(k), span(j)]
+            elif j > k:
+                factor, back = work[span(k), span(j)], zero
+            else:
+                factor = jnp.where(col_at >= row_at, upper_ref[k % 2], 0.0)
+                back = inverse_ref[k % 2]
+            factor_ref[span(k), span(j)] = factor * (1.0 / total_scale)
+            high, low = split(back * total_scale)
+            high_ref[span(k), span(j)] = high
+            low_ref[span(k), span(j)] = low
+
+    def below(k, i, left, right, first):
+        change = parts_dot(left, [r[:, : LANES * (k + 1)] for r in right])
+        if k:
+            work[span(i), span(0, k)] = work[span(i), span(0, k)] - change[:, : LANES * k]
+        work[span(i), span(k)] = -change[:, LANES * k :]
+        if first < blocks:
+            cols = span(first, blocks)
+            work[span(i), cols] = work[span(i), cols] - parts_dot(
+                left, [r[:, cols] for r in right]
             )
-            return 0
-
-        lax.fori_loop(k + 1, blocks, below, 0)
-        return 0
-
-    lax.fori_loop(0, blocks, stage, 0)
+
+    def later(k, left, solved, turned):
+        row = {}
+
+        def solve_rest():
+            if k:
+                cols = span(0, k)
+                work[span(k), cols] = parts_dot(left, right_parts(work[span(k), cols]))
+            if k + 2 < blocks:
+                cols = span(k + 2, blocks)
+                work[span(k), cols] = parts_dot(left, right_parts(work[span(k), cols]))
+            if k + 1 < blocks:
+                work[span(k), span(k + 1)] = solved
+            row["parts"] = right_parts(
+                jnp.concatenate(
+                    [
+                        inverse_ref[k % 2] if j == k else work[span(k), span(j)]
+                        for j in range(blocks)
+                    ],
+                    axis=1,
+                )
+            )
+
+        todo = [solve_rest]
+        for i in range(k + 1, blocks):
+
+            def one(i=i):
+                lead = turned if i == k + 1 else left_parts(work[span(k), span(i)].T)
+                below(k, i, lead, row["parts"], max(i, k + 2))
+
+            todo.append(one)
+        todo.append(lambda: write_row(k))
+        return todo
+
+    gather(0, 0, 1)
+    todo = [lambda: gather(0, 1, blocks)]
+    todo += [lambda i=i: gather(i, i, blocks) for i in range(1, blocks)]
+    for k in range(blocks):
+        groups = LANES // SUB
+        done = 0
+        steps = factor_block(work[span(k), span(k)], upper_ref.at[k % 2], inverse_ref.at[k % 2])
+        for g, _ in enumerate(steps):
+            due = -(-len(todo) * (g + 1) // groups)
+            for piece in todo[done:due]:
+                piece()
+            done = due
+        left = left_parts(inverse_ref[k % 2])
+        solved = turned = None
+        if k + 1 < blocks:
+            solved = parts_dot(left, right_parts(work[span(k), span(k + 1)]))
+            turned = left_parts(solved.T)
+            work[span(k + 1), span(k + 1)] = work[span(k + 1), span(k + 1)] - parts_dot(
+                turned, right_parts(solved)
+            )
+        todo = later(k, left, solved, turned)
+    for piece in todo:
+        piece()
 
 
 def factor_and_inverse(held, other, numbers, piece_rows, width, local_rows):
@@ -279,8 +372,8 @@
             pltpu.VMEM((width, width), jnp.float32),
             pltpu.VMEM((pieces * piece_rows, LANES), jnp.float32),
             pltpu.VMEM((pieces * SUB, LANES), jnp.float32),
-            pltpu.VMEM((LANES, LANES), jnp.float32),
-            pltpu.VMEM((LANES, LANES), jnp.float32),
+            pltpu.VMEM((2, LANES, LANES), jnp.float32),
+            pltpu.VMEM((2, LANES, LANES), jnp.float32),
         ],
         compiler_params=pltpu.CompilerParams(vmem_limit_bytes=48 * 2**20),
     )(held, other, numbers, counts)

time: 120 us -> 98.8 us (0.82)
  Pallas kernels: 63.6 us -> 42 us
    pallas_call x1, Pallas kernels: 49.9 us -> 28.3 us  [factor_and_inverse(): pl.pallas_call(factor_kernel, out_shape=(jax.ShapeDtypeStruct((width, wid...]
where the time goes in v3:
time: 98.8 us; the launch traced here: 98.5 us
  Pallas kernels  42 us (43%)
  waiting for transfers between devices  32.2 us (33%)
  starting transfers between devices  20.7 us (21%)
  local copies, waits for them, and re-layouts  2.54 us (3%)
    pallas_call x1, Pallas kernels, factor_and_inverse(): pl.pallas_call(factor_kernel, out_shape=(jax.ShapeDtypeStruct((width, wid...  28.3 us
    ppermute x5, waiting for transfers between devices, sum_in_pieces(): other = lax.ppermute(held, AXES, partners(step))  16.9 us
    ppermute x5, waiting for transfers between devices, sum_in_pieces(): piece = kept + lax.ppermute(sent, AXES, partners(step))  15.3 us
    ppermute x5, starting transfers between devices, sum_in_pieces(): piece = kept + lax.ppermute(sent, AXES, partners(step))  10.7 us
    ppermute x5, starting transfers between devices, sum_in_pieces(): other = lax.ppermute(held, AXES, partners(step))  9.92 us
    pallas_call x1, Pallas kernels, whiten(): pl.pallas_call(whiten_kernel, grid=(rows // TILE,), out_shape=jax.ShapeDt...  8.29 us
    pallas_call x1, Pallas kernels, local_gram(): pl.pallas_call(gram_kernel, out_shape=(jax.ShapeDtypeStruct((packed_rows,...  5.41 us
    unnamed x7, local copies, waits for them, and re-layouts  2.37 us
  transfers between devices with their start and end apart: 10, of which 10 were waited for; matrix products, arithmetic and copies ran while one was open for 0% of the time, Pallas kernels for 0%

profile of v3, /device:TPU:0, one launch (start us, length us, event | category | flops | bytes accessed | tf_op | source)
XLA Modules:
  0.0 98.5 jit_solution(6227457010718008925)
XLA Ops:
  0.6 0.0 copy-start
  0.6 2.3 %copy-done = f32[1536,768]{1,0:T(8,128)S(1)} copy-done((f32[1536,768]{1,0:T(8,128)S(1)}, f32[1536,768]{1,0:T(8,128)}, u32[]{:S(2)}) %copy-start) | copy-done | bytes 4718616
  3.0 5.4 %shard_map.41 = (f32[2816,128]{1,0:T(8,128)S(1)}, f32[8,128]{1,0:T(8,128)S(1)}) custom-call(f32[1536,768]{1,0:T(8,128)S(1)} %copy-done), custom_call_target="tpu_custom_call" | custom-call | tf_op jit(solution)/shard_map/pallas_call | solution.py:81
  8.4 0.1 constant_dynamic-slice_fusion.4
  8.5 0.5 collective-permute-start
  9.0 1.8 %collective-permute-done = f32[1408,128]{1,0:T(8,128)S(1)} collective-permute-done((f32[1408,128]{1,0:T(8,128)S(1)}, f32[1408,128]{1,0:T(8,128)S(1)}, u32[]{:S(2)}, u32[]{:S(2)}) %collective-permute-start) | collective-permute-done | bytes 720928 | tf_op jit(solution)/shard_map/ppermute | solution.py:123
  10.8 0.1 dynamic-slice_add_fusion
  10.9 2.9 %collective-permute-start.1 = (f32[704,128]{1,0:T(8,128)S(1)}, f32[704,128]{1,0:T(8,128)S(1)}, u32[]{:S(2)}, u32[]{:S(2)}) collective-permute-start(f32[704,128]{1,0:T(8,128)S(1)} %constant_dynamic-slice_fusion.3), channel_id=1, source_target_pairs={{0,8},{1,17},{2,10},{3,19},{4,12},{5,21},{6,14},{7,23},{8,0},{9,25... | collective-permute-start | bytes 1081352 | tf_op jit(solution)/shard_map/ppermute | solution.py:123
  13.9 5.4 %collective-permute-done.1 = f32[704,128]{1,0:T(8,128)S(1)} collective-permute-done((f32[704,128]{1,0:T(8,128)S(1)}, f32[704,128]{1,0:T(8,128)S(1)}, u32[]{:S(2)}, u32[]{:S(2)}) %collective-permute-start.1) | collective-permute-done | bytes 360480 | tf_op jit(solution)/shard_map/ppermute | solution.py:123
  19.3 2.2 %collective-permute-start.2 = (f32[352,128]{1,0:T(8,128)S(1)}, f32[352,128]{1,0:T(8,128)S(1)}, u32[]{:S(2)}, u32[]{:S(2)}) collective-permute-start(f32[352,128]{1,0:T(8,128)S(1)} %constant_dynamic-slice_fusion.2), channel_id=1, source_target_pairs={{0,2},{1,9},{2,0},{3,11},{4,6},{5,13},{6,4},{7,15},{8,10},{9,1},{1... | collective-permute-start | bytes 540680 | tf_op jit(solution)/shard_map/ppermute | solution.py:123
  21.5 3.5 %collective-permute-done.2 = f32[352,128]{1,0:T(8,128)S(1)} collective-permute-done((f32[352,128]{1,0:T(8,128)S(1)}, f32[352,128]{1,0:T(8,128)S(1)}, u32[]{:S(2)}, u32[]{:S(2)}) %collective-permute-start.2) | collective-permute-done | bytes 180256 | tf_op jit(solution)/shard_map/ppermute | solution.py:123
  25.0 2.0 %collective-permute-start.3 = (f32[176,128]{1,0:T(8,128)S(1)}, f32[176,128]{1,0:T(8,128)S(1)}, u32[]{:S(2)}, u32[]{:S(2)}) collective-permute-start(f32[176,128]{1,0:T(8,128)S(1)} %constant_dynamic-slice_fusion.1), channel_id=1, source_target_pairs={{0,16},{1,3},{2,18},{3,1},{4,20},{5,7},{6,22},{7,5},{8,24},{9,11},... | collective-permute-start | bytes 270344 | tf_op jit(solution)/shard_map/ppermute | solution.py:123
  27.1 2.6 %collective-permute-done.3 = f32[176,128]{1,0:T(8,128)S(1)} collective-permute-done((f32[176,128]{1,0:T(8,128)S(1)}, f32[176,128]{1,0:T(8,128)S(1)}, u32[]{:S(2)}, u32[]{:S(2)}) %collective-permute-start.3) | collective-permute-done | bytes 90144 | tf_op jit(solution)/shard_map/ppermute | solution.py:123
  29.7 3.1 %collective-permute-start.4 = (f32[88,128]{1,0:T(8,128)S(1)}, f32[88,128]{1,0:T(8,128)S(1)}, u32[]{:S(2)}, u32[]{:S(2)}) collective-permute-start(f32[88,128]{1,0:T(8,128)S(1)} %constant_dynamic-slice_fusion), channel_id=1, source_target_pairs={{0,4},{1,5},{2,6},{3,7},{4,0},{5,1},{6,2},{7,3},{8,12},{9,13},{10,... | collective-permute-start | bytes 135176 | tf_op jit(solution)/shard_map/ppermute | solution.py:123
  32.8 2.0 %collective-permute-done.4 = f32[88,128]{1,0:T(8,128)S(1)} collective-permute-done((f32[88,128]{1,0:T(8,128)S(1)}, f32[88,128]{1,0:T(8,128)S(1)}, u32[]{:S(2)}, u32[]{:S(2)}) %collective-permute-start.4) | collective-permute-done | bytes 45088 | tf_op jit(solution)/shard_map/ppermute | solution.py:123
  34.8 3.3 %collective-permute-start.5 = (f32[1,96,128]{2,1,0:T(8,128)S(1)}, f32[1,96,128]{2,1,0:T(8,128)S(1)}, u32[]{:S(2)}, u32[]{:S(2)}) collective-permute-start(f32[1,96,128]{2,1,0:T(8,128)S(1)} %maximum_bitcast_fusion), channel_id=1, source_target_pairs={{0,4},{1,5},{2,6},{3,7},{4,0},{5,1},{6,2},{7,3},{8,12},{9,13},{10,... | collective-permute-start | bytes 147464 | tf_op jit(solution)/shard_map/ppermute | solution.py:126
  38.1 2.1 %collective-permute-done.5 = f32[1,96,128]{2,1,0:T(8,128)S(1)} collective-permute-done((f32[1,96,128]{2,1,0:T(8,128)S(1)}, f32[1,96,128]{2,1,0:T(8,128)S(1)}, u32[]{:S(2)}, u32[]{:S(2)}) %collective-permute-start.5) | collective-permute-done | bytes 49184 | tf_op jit(solution)/shard_map/ppermute | solution.py:126
  40.2 0.0 copy-start.1
  40.2 1.9 %collective-permute-start.6 = (f32[2,96,128]{2,1,0:T(8,128)S(1)}, f32[2,96,128]{2,1,0:T(8,128)S(1)}, u32[]{:S(2)}, u32[]{:S(2)}) collective-permute-start(f32[2,96,128]{2,1,0:T(8,128)S(1)} %pad_maximum_fusion.2), channel_id=1, source_target_pairs={{0,16},{1,3},{2,18},{3,1},{4,20},{5,7},{6,22},{7,5},{8,24},{9,11},... | collective-permute-start | bytes 294920 | tf_op jit(solution)/shard_map/ppermute | solution.py:126
  42.1 2.8 %collective-permute-done.6 = f32[2,96,128]{2,1,0:T(8,128)S(1)} collective-permute-done((f32[2,96,128]{2,1,0:T(8,128)S(1)}, f32[2,96,128]{2,1,0:T(8,128)S(1)}, u32[]{:S(2)}, u32[]{:S(2)}) %collective-permute-start.6) | collective-permute-done | bytes 98336 | tf_op jit(solution)/shard_map/ppermute | solution.py:126
  44.9 3.1 %collective-permute-start.7 = (f32[4,96,128]{2,1,0:T(8,128)S(1)}, f32[4,96,128]{2,1,0:T(8,128)S(1)}, u32[]{:S(2)}, u32[]{:S(2)}) collective-permute-start(f32[4,96,128]{2,1,0:T(8,128)S(1)} %pad_maximum_fusion.1), channel_id=1, source_target_pairs={{0,2},{1,9},{2,0},{3,11},{4,6},{5,13},{6,4},{7,15},{8,10},{9,1},{1... | collective-permute-start | bytes 589832 | tf_op jit(solution)/shard_map/ppermute | solution.py:126
  48.0 3.6 %collective-permute-done.7 = f32[4,96,128]{2,1,0:T(8,128)S(1)} collective-permute-done((f32[4,96,128]{2,1,0:T(8,128)S(1)}, f32[4,96,128]{2,1,0:T(8,128)S(1)}, u32[]{:S(2)}, u32[]{:S(2)}) %collective-permute-start.7) | collective-permute-done | bytes 196640 | tf_op jit(solution)/shard_map/ppermute | solution.py:126
  51.7 1.6 %collective-permute-start.8 = (f32[8,96,128]{2,1,0:T(8,128)S(1)}, f32[8,96,128]{2,1,0:T(8,128)S(1)}, u32[]{:S(2)}, u32[]{:S(2)}) collective-permute-start(f32[8,96,128]{2,1,0:T(8,128)S(1)} %pad_maximum_fusion), channel_id=1, source_target_pairs={{0,8},{1,17},{2,10},{3,19},{4,12},{5,21},{6,14},{7,23},{8,0},{9,25... | collective-permute-start | bytes 1179656 | tf_op jit(solution)/shard_map/ppermute | solution.py:126
  53.3 6.2 %collective-permute-done.8 = f32[8,96,128]{2,1,0:T(8,128)S(1)} collective-permute-done((f32[8,96,128]{2,1,0:T(8,128)S(1)}, f32[8,96,128]{2,1,0:T(8,128)S(1)}, u32[]{:S(2)}, u32[]{:S(2)}) %collective-permute-start.8) | collective-permute-done | bytes 393248 | tf_op jit(solution)/shard_map/ppermute | solution.py:126
  59.6 0.1 collective-permute-start.9
  59.7 0.1 pad_add_fusion.numbers_ref
  59.8 2.2 %collective-permute-done.9.other_ref = f32[16,96,128]{2,1,0:T(8,128)S(1)} collective-permute-done((f32[16,96,128]{2,1,0:T(8,128)S(1)}, f32[16,96,128]{2,1,0:T(8,128)S(1)}, u32[]{:S(2)}, u32[]{:S(2)}) %collective-permute-start.9) | collective-permute-done | bytes 786464 | tf_op jit(solution)/shard_map/ppermute | solution.py:126
  61.9 0.0 copy-done.1
  61.9 28.3 %shard_map.42 = (f32[768,768]{1,0:T(8,128)}, bf16[768,768]{1,0:T(8,128)(2,1)S(1)}, bf16[768,768]{1,0:T(8,128)(2,1)S(1)}, f32[8,768]{1,0:T(8,128)S(1)}) custom-call(f32[16,96,128]{2,1,0:T(8,128)S(1)} %constant_dynamic-update-slice_fusion.held_ref, f32[16,96,128]{2,1,0:T(8,128)S(1)} %collective-permute-done.9.other_ref, s32[2]{0:T(128)S(1)} %pad_add_fusion.numbers_ref, ...), custom_call_target="tpu_custom_call" | custom-call | tf_op jit(solution)/shard_map/pallas_call | solution.py:361
  90.2 8.3 %shard_map.43 = f32[1536,768]{1,0:T(8,128)} custom-call(f32[1536,768]{1,0:T(8,128)} %x_ref.3, f32[8,768]{1,0:T(8,128)S(1)} %get-tuple-element.10.mean_ref, bf16[768,768]{1,0:T(8,128)(2,1)S(1)} %get-tuple-element.11.high_ref, bf16[768,768]{1,0:T(8,128)(2,1)S(1)} %get-tuple-element.12.low_ref), custom_call_target="tpu_custom_call" | custom-call | tf_op jit(solution)/shard_map/pallas_call | solution.py:396
  (17 shorter events, 0.3 us)
Async XLA Ops:
  0.6 2.3 %copy-start = (f32[1536,768]{1,0:T(8,128)S(1)}, f32[1536,768]{1,0:T(8,128)}, u32[]{:S(2)}) copy-start(f32[1536,768]{1,0:T(8,128)} %x_ref.3) | copy-start | bytes 14155780
  8.5 2.3 %collective-permute-start = (f32[1408,128]{1,0:T(8,128)S(1)}, f32[1408,128]{1,0:T(8,128)S(1)}, u32[]{:S(2)}, u32[]{:S(2)}) collective-permute-start(f32[1408,128]{1,0:T(8,128)S(1)} %constant_dynamic-slice_fusion.4), channel_id=1, source_target_pairs={{0,1},{1,0},{2,3},{3,2},{4,5},{5,4},{6,7},{7,6},{8,9},{9,8},{10,11... | collective-permute-start | bytes 2162696 | tf_op jit(solution)/shard_map/ppermute | solution.py:123
  10.9 8.3 %collective-permute-start.1 = (f32[704,128]{1,0:T(8,128)S(1)}, f32[704,128]{1,0:T(8,128)S(1)}, u32[]{:S(2)}, u32[]{:S(2)}) collective-permute-start(f32[704,128]{1,0:T(8,128)S(1)} %constant_dynamic-slice_fusion.3), channel_id=1, source_target_pairs={{0,8},{1,17},{2,10},{3,19},{4,12},{5,21},{6,14},{7,23},{8,0},{9,25... | collective-permute-start | bytes 1081352 | tf_op jit(solution)/shard_map/ppermute | solution.py:123
  19.3 5.6 %collective-permute-start.2 = (f32[352,128]{1,0:T(8,128)S(1)}, f32[352,128]{1,0:T(8,128)S(1)}, u32[]{:S(2)}, u32[]{:S(2)}) collective-permute-start(f32[352,128]{1,0:T(8,128)S(1)} %constant_dynamic-slice_fusion.2), channel_id=1, source_target_pairs={{0,2},{1,9},{2,0},{3,11},{4,6},{5,13},{6,4},{7,15},{8,10},{9,1},{1... | collective-permute-start | bytes 540680 | tf_op jit(solution)/shard_map/ppermute | solution.py:123
  25.0 4.6 %collective-permute-start.3 = (f32[176,128]{1,0:T(8,128)S(1)}, f32[176,128]{1,0:T(8,128)S(1)}, u32[]{:S(2)}, u32[]{:S(2)}) collective-permute-start(f32[176,128]{1,0:T(8,128)S(1)} %constant_dynamic-slice_fusion.1), channel_id=1, source_target_pairs={{0,16},{1,3},{2,18},{3,1},{4,20},{5,7},{6,22},{7,5},{8,24},{9,11},... | collective-permute-start | bytes 270344 | tf_op jit(solution)/shard_map/ppermute | solution.py:123
  29.7 5.1 %collective-permute-start.4 = (f32[88,128]{1,0:T(8,128)S(1)}, f32[88,128]{1,0:T(8,128)S(1)}, u32[]{:S(2)}, u32[]{:S(2)}) collective-permute-start(f32[88,128]{1,0:T(8,128)S(1)} %constant_dynamic-slice_fusion), channel_id=1, source_target_pairs={{0,4},{1,5},{2,6},{3,7},{4,0},{5,1},{6,2},{7,3},{8,12},{9,13},{10,... | collective-permute-start | bytes 135176 | tf_op jit(solution)/shard_map/ppermute | solution.py:123
  34.8 5.4 %collective-permute-start.5 = (f32[1,96,128]{2,1,0:T(8,128)S(1)}, f32[1,96,128]{2,1,0:T(8,128)S(1)}, u32[]{:S(2)}, u32[]{:S(2)}) collective-permute-start(f32[1,96,128]{2,1,0:T(8,128)S(1)} %maximum_bitcast_fusion), channel_id=1, source_target_pairs={{0,4},{1,5},{2,6},{3,7},{4,0},{5,1},{6,2},{7,3},{8,12},{9,13},{10,... | collective-permute-start | bytes 147464 | tf_op jit(solution)/shard_map/ppermute | solution.py:126
  40.2 21.7 %copy-start.1 = (f32[2]{0:T(128)S(1)}, f32[2]{0:T(128)}, u32[]{:S(2)}) copy-start(f32[2]{0:T(128)} %constant.34.clone.count_ref) | copy-start | bytes 28
  40.2 4.7 %collective-permute-start.6 = (f32[2,96,128]{2,1,0:T(8,128)S(1)}, f32[2,96,128]{2,1,0:T(8,128)S(1)}, u32[]{:S(2)}, u32[]{:S(2)}) collective-permute-start(f32[2,96,128]{2,1,0:T(8,128)S(1)} %pad_maximum_fusion.2), channel_id=1, source_target_pairs={{0,16},{1,3},{2,18},{3,1},{4,20},{5,7},{6,22},{7,5},{8,24},{9,11},... | collective-permute-start | bytes 294920 | tf_op jit(solution)/shard_map/ppermute | solution.py:126
  44.9 6.8 %collective-permute-start.7 = (f32[4,96,128]{2,1,0:T(8,128)S(1)}, f32[4,96,128]{2,1,0:T(8,128)S(1)}, u32[]{:S(2)}, u32[]{:S(2)}) collective-permute-start(f32[4,96,128]{2,1,0:T(8,128)S(1)} %pad_maximum_fusion.1), channel_id=1, source_target_pairs={{0,2},{1,9},{2,0},{3,11},{4,6},{5,13},{6,4},{7,15},{8,10},{9,1},{1... | collective-permute-start | bytes 589832 | tf_op jit(solution)/shard_map/ppermute | solution.py:126
  51.7 7.8 %collective-permute-start.8 = (f32[8,96,128]{2,1,0:T(8,128)S(1)}, f32[8,96,128]{2,1,0:T(8,128)S(1)}, u32[]{:S(2)}, u32[]{:S(2)}) collective-permute-start(f32[8,96,128]{2,1,0:T(8,128)S(1)} %pad_maximum_fusion), channel_id=1, source_target_pairs={{0,8},{1,17},{2,10},{3,19},{4,12},{5,21},{6,14},{7,23},{8,0},{9,25... | collective-permute-start | bytes 1179656 | tf_op jit(solution)/shard_map/ppermute | solution.py:126
  59.6 2.4 %collective-permute-start.9 = (f32[16,96,128]{2,1,0:T(8,128)S(1)}, f32[16,96,128]{2,1,0:T(8,128)S(1)}, u32[]{:S(2)}, u32[]{:S(2)}) collective-permute-start(f32[16,96,128]{2,1,0:T(8,128)S(1)} %constant_dynamic-update-slice_fusion.held_ref), channel_id=1, source_target_pairs={{0,1},{1,0},{2,3},{3,2},{4,5},{5,4},{6,7},{7,6},{8,9},{9,8},{10,11... | collective-permute-start | bytes 2359304 | tf_op jit(solution)/shard_map/ppermute | solution.py:126

commit v4 on v3

--- a/solution.py
+++ b/solution.py
@@ -91,42 +91,34 @@
     )(embeddings)
 
 
-def exchange_orders(bits):
-    body = [b for b in (3, 1) + tuple(range(4, bits)) if b < bits]
-    tail = [2] if bits > 2 else []
-    return [0] + body + tail, [0] + body[-1:] + body[:-1] + tail
-
-
 def sum_in_pieces(packed, mean_rows):
-    devices = lax.axis_size("grp") * lax.axis_size("wide")
-    bits = devices.bit_length() - 1
-    orders = exchange_orders(bits)
-    me = lax.axis_index(AXES)
-    on_core = me & 1
-
-    def partners(step):
-        return [(d, d ^ (1 << orders[d & 1][step])) for d in range(devices)]
-
-    def bit_at(step, core):
-        return jnp.where(core == 0, me >> orders[0][step], me >> orders[1][step]) & 1
-
-    mine, twin = on_core, 1 - on_core
-    for step in range(1, bits):
-        mine = mine * 2 + bit_at(step, on_core)
-        twin = twin * 2 + bit_at(step, 1 - on_core)
-    piece = packed
-    for step in range(bits):
-        bit = bit_at(step, on_core)
-        half = piece.shape[0] // 2
-        sent = lax.dynamic_slice_in_dim(piece, (1 - bit) * half, half, 0)
-        kept = lax.dynamic_slice_in_dim(piece, bit * half, half, 0)
-        piece = kept + lax.ppermute(sent, AXES, partners(step))
-    held = jnp.concatenate([piece, mean_rows], axis=0)[None]
-    for step in reversed(range(bits)):
-        other = lax.ppermute(held, AXES, partners(step))
-        if step:
-            held = jnp.concatenate([held, other], axis=0)
-    return held, other, jnp.stack([mine, twin])
+    groups, wide = lax.axis_size("grp"), lax.axis_size("wide")
+    core = lax.axis_index("wide") & 1
+    twins = [(d, d ^ 1) for d in range(wide)]
+    same_core = [list(range(c, wide, 2)) for c in range(2)]
+
+    def over_grp(parts):
+        return lax.all_to_all(parts, "grp", 0, 0)
+
+    def over_wide(parts):
+        return lax.all_to_all(parts, "wide", 0, 0, axis_index_groups=same_core)
+
+    def spread(parts, trade, count):
+        return trade(jnp.broadcast_to(parts[None], (count,) + parts.shape))
+
+    half = packed.shape[0] // 2
+    sent = lax.dynamic_slice_in_dim(packed, (1 - core) * half, half, 0)
+    kept = lax.dynamic_slice_in_dim(packed, core * half, half, 0)
+    piece = kept + lax.ppermute(sent, "wide", twins)
+    piece = jnp.sum(over_grp(piece.reshape(groups, -1, LANES)), axis=0)
+    piece = jnp.sum(over_wide(piece.reshape(wide // 2, -1, LANES)), axis=0)
+    held = jnp.concatenate([piece, mean_rows], axis=0)
+    held = spread(held, over_wide, wide // 2)
+    held = spread(held, over_grp, groups)
+    held = held.reshape((-1,) + held.shape[2:])
+    other = lax.ppermute(held, "wide", twins)
+    half = held.shape[0]
+    return held, other, jnp.stack([core * half, (1 - core) * half])
 
 
 def factor_block(block, upper_ref, inverse_ref):

time: 98.8 us -> 97.7 us (0.989)
  blocking collectives: 0 us -> 47.5 us
  waiting for transfers between devices: 32.2 us -> 4.03 us
  starting transfers between devices: 20.7 us -> 0.52 us
    all_to_all x0 -> x4, blocking collectives: none -> 47.5 us  [the longest x2 26.9 us: over_grp(): return lax.all_to_all(parts, 'grp', 0, 0)]
    ppermute x10 -> x2, waiting for transfers between devices: 32.2 us -> 4.03 us  [the longest x1 2.21 us: sum_in_pieces(): other = lax.ppermute(held, 'wide', twins)]
    ppermute x10 -> x2, starting transfers between devices: 20.7 us -> 0.52 us  [the longest x1 0.52 us: sum_in_pieces(): piece = kept + lax.ppermute(sent, 'wide', twins)]
    unnamed x7 -> x4, local copies, waits for them, and re-layouts: 2.37 us -> 2.34 us
  transfers between devices with their start and end apart: 10 -> 2, of which waited for: 10 -> 2; matrix products, arithmetic and copies ran while one was open for 0% -> 0% of each run, Pallas kernels for 0% -> 0%
where the time goes in v4:
time: 97.7 us; the launch traced here: 97.3 us
  blocking collectives  47.5 us (49%)
  Pallas kernels  41.8 us (43%)
  waiting for transfers between devices  4.03 us (4%)
  local copies, waits for them, and re-layouts  2.48 us (3%)
    pallas_call x1, Pallas kernels, factor_and_inverse(): pl.pallas_call(factor_kernel, out_shape=(jax.ShapeDtypeStruct((width, wid...  28.1 us
    all_to_all x2, blocking collectives, over_grp(): return lax.all_to_all(parts, 'grp', 0, 0)  26.9 us
    all_to_all x2, blocking collectives, over_wide(): return lax.all_to_all(parts, 'wide', 0, 0, axis_index_groups=same_core)  20.6 us
    pallas_call x1, Pallas kernels, whiten(): pl.pallas_call(whiten_kernel, grid=(rows // TILE,), out_shape=jax.ShapeDt...  8.29 us
    pallas_call x1, Pallas kernels, local_gram(): pl.pallas_call(gram_kernel, out_shape=(jax.ShapeDtypeStruct((packed_rows,...  5.41 us
    unnamed x4, local copies, waits for them, and re-layouts  2.34 us
    ppermute x1, waiting for transfers between devices, sum_in_pieces(): other = lax.ppermute(held, 'wide', twins)  2.21 us
  transfers between devices with their start and end apart: 2, of which 2 were waited for; matrix products, arithmetic and copies ran while one was open for 0% of the time, Pallas kernels for 0%

profile of v4, /device:TPU:0, one launch (start us, length us, event | category | flops | bytes accessed | tf_op | source)
XLA Modules:
  0.0 97.3 jit_solution(818770874059894929)
XLA Ops:
  0.6 0.0 copy-start
  0.6 2.3 %copy-done = f32[1536,768]{1,0:T(8,128)S(1)} copy-done((f32[1536,768]{1,0:T(8,128)S(1)}, f32[1536,768]{1,0:T(8,128)}, u32[]{:S(2)}) %copy-start) | copy-done | bytes 4718616
  3.0 5.4 %shard_map.41 = (f32[2816,128]{1,0:T(8,128)S(1)}, f32[8,128]{1,0:T(8,128)S(1)}) custom-call(f32[1536,768]{1,0:T(8,128)S(1)} %copy-done), custom_call_target="tpu_custom_call" | custom-call | tf_op jit(solution)/shard_map/pallas_call | solution.py:81
  8.4 0.1 constant_dynamic-slice_fusion
  8.5 0.5 collective-permute-start
  9.0 1.8 %collective-permute-done = f32[1408,128]{1,0:T(8,128)S(1)} collective-permute-done((f32[1408,128]{1,0:T(8,128)S(1)}, f32[1408,128]{1,0:T(8,128)S(1)}, u32[]{:S(2)}, u32[]{:S(2)}) %collective-permute-start) | collective-permute-done | bytes 720928 | tf_op jit(solution)/shard_map/ppermute | solution.py:112
  10.8 0.1 dynamic-slice_add_fusion
  10.9 16.0 %all_to_all.20 = f32[4,352,128]{2,1,0:T(8,128)S(1)} all-to-all(f32[4,352,128]{2,1,0:T(8,128)S(1)} %bitcast.7), channel_id=1, replica_groups=mesh['grp'=4,'wide'=8] {'grp'}, dimensions={0} | all-to-all | bytes 1441792 | tf_op jit(solution)/shard_map/all_to_all | solution.py:101
  26.9 11.4 %all_to_all.21 = f32[4,88,128]{2,1,0:T(8,128)S(1)} all-to-all(f32[4,88,128]{2,1,0:T(8,128)S(1)} %bitcast.8), channel_id=1, replica_groups={{0,2,4,6},{1,3,5,7},{8,10,12,14},{9,11,13,15},{16,18,20,22},{17,19,21,2..., dimensions={0} | all-to-all | bytes 360448 | tf_op jit(solution)/shard_map/all_to_all | solution.py:104
  38.4 0.0 copy-start.1
  38.4 9.2 %all_to_all.22 = f32[4,96,128]{2,1,0:T(8,128)S(1)} all-to-all(f32[4,96,128]{2,1,0:T(8,128)S(1)} %broadcast_in_dim.4), channel_id=1, replica_groups={{0,2,4,6},{1,3,5,7},{8,10,12,14},{9,11,13,15},{16,18,20,22},{17,19,21,2..., dimensions={0} | all-to-all | bytes 393216 | tf_op jit(solution)/shard_map/all_to_all | solution.py:104
  47.6 0.1 broadcast_in_dim.5
  47.7 10.9 %all_to_all.23 = f32[4,4,96,128]{3,2,1,0:T(8,128)S(1)} all-to-all(f32[4,4,96,128]{3,2,1,0:T(8,128)S(1)} %broadcast_in_dim.5), channel_id=1, replica_groups=mesh['grp'=4,'wide'=8] {'grp'}, dimensions={0} | all-to-all | bytes 1572864 | tf_op jit(solution)/shard_map/all_to_all | solution.py:101
  58.6 0.0 collective-permute-start.1
  58.6 0.1 pad_add_fusion.numbers_ref
  58.7 2.2 %collective-permute-done.1.other_ref = f32[16,96,128]{2,1,0:T(8,128)S(1)} collective-permute-done((f32[16,96,128]{2,1,0:T(8,128)S(1)}, f32[16,96,128]{2,1,0:T(8,128)S(1)}, u32[]{:S(2)}, u32[]{:S(2)}) %collective-permute-start.1) | collective-permute-done | bytes 786464 | tf_op jit(solution)/shard_map/ppermute | solution.py:119
  60.9 0.0 copy-done.1
  60.9 28.1 %shard_map.42 = (f32[768,768]{1,0:T(8,128)}, bf16[768,768]{1,0:T(8,128)(2,1)S(1)}, bf16[768,768]{1,0:T(8,128)(2,1)S(1)}, f32[8,768]{1,0:T(8,128)S(1)}) custom-call(f32[16,96,128]{2,1,0:T(8,128)S(1)} %bitcast.6, f32[16,96,128]{2,1,0:T(8,128)S(1)} %collective-permute-done.1.other_ref, s32[2]{0:T(128)S(1)} %pad_add_fusion.numbers_ref, f32[2]{0:T(128)S(1)} %copy-done.1), custom_call_target="tpu_custom_call" | custom-call | tf_op jit(solution)/shard_map/pallas_call | solution.py:353
  89.0 8.3 %shard_map.43 = f32[1536,768]{1,0:T(8,128)} custom-call(f32[1536,768]{1,0:T(8,128)} %x_ref.3, f32[8,768]{1,0:T(8,128)S(1)} %get-tuple-element.10.mean_ref, bf16[768,768]{1,0:T(8,128)(2,1)S(1)} %get-tuple-element.11.high_ref, bf16[768,768]{1,0:T(8,128)(2,1)S(1)} %get-tuple-element.12.low_ref), custom_call_target="tpu_custom_call" | custom-call | tf_op jit(solution)/shard_map/pallas_call | solution.py:388
  (4 shorter events, 0.1 us)
Async XLA Ops:
  0.6 2.3 %copy-start = (f32[1536,768]{1,0:T(8,128)S(1)}, f32[1536,768]{1,0:T(8,128)}, u32[]{:S(2)}) copy-start(f32[1536,768]{1,0:T(8,128)} %x_ref.3) | copy-start | bytes 14155780
  8.5 2.3 %collective-permute-start = (f32[1408,128]{1,0:T(8,128)S(1)}, f32[1408,128]{1,0:T(8,128)S(1)}, u32[]{:S(2)}, u32[]{:S(2)}) collective-permute-start(f32[1408,128]{1,0:T(8,128)S(1)} %constant_dynamic-slice_fusion), channel_id=1, source_target_pairs={{0,1},{1,0},{2,3},{3,2},{4,5},{5,4},{6,7},{7,6},{8,9},{9,8},{10,11... | collective-permute-start | bytes 2162696 | tf_op jit(solution)/shard_map/ppermute | solution.py:112
  38.4 22.5 %copy-start.1 = (f32[2]{0:T(128)S(1)}, f32[2]{0:T(128)}, u32[]{:S(2)}) copy-start(f32[2]{0:T(128)} %constant.18.clone.count_ref) | copy-start | bytes 28
  58.6 2.3 %collective-permute-start.1 = (f32[16,96,128]{2,1,0:T(8,128)S(1)}, f32[16,96,128]{2,1,0:T(8,128)S(1)}, u32[]{:S(2)}, u32[]{:S(2)}) collective-permute-start(f32[16,96,128]{2,1,0:T(8,128)S(1)} %bitcast.5), channel_id=1, source_target_pairs={{0,1},{1,0},{2,3},{3,2},{4,5},{5,4},{6,7},{7,6},{8,9},{9,8},{10,11... | collective-permute-start | bytes 2359304 | tf_op jit(solution)/shard_map/ppermute | solution.py:119

commit v5 on v3

--- a/solution.py
+++ b/solution.py
@@ -98,35 +98,39 @@
 
 
 def sum_in_pieces(packed, mean_rows):
-    devices = lax.axis_size("grp") * lax.axis_size("wide")
+    groups, wide = lax.axis_size("grp"), lax.axis_size("wide")
+    devices = groups * wide
     bits = devices.bit_length() - 1
     orders = exchange_orders(bits)
     me = lax.axis_index(AXES)
-    on_core = me & 1
-
-    def partners(step):
-        return [(d, d ^ (1 << orders[d & 1][step])) for d in range(devices)]
-
-    def bit_at(step, core):
-        return jnp.where(core == 0, me >> orders[0][step], me >> orders[1][step]) & 1
-
-    mine, twin = on_core, 1 - on_core
-    for step in range(1, bits):
-        mine = mine * 2 + bit_at(step, on_core)
-        twin = twin * 2 + bit_at(step, 1 - on_core)
+    core = me & 1
+    twins = [(d, d ^ 1) for d in range(wide)]
+    same_core = [list(range(c, wide, 2)) for c in range(2)]
+
+    def number(device):
+        order = orders[device & 1]
+        return sum(((device >> b) & 1) << (bits - 1 - step) for step, b in enumerate(order))
+
     piece = packed
     for step in range(bits):
-        bit = bit_at(step, on_core)
+        bit = jnp.where(core == 0, me >> orders[0][step], me >> orders[1][step]) & 1
         half = piece.shape[0] // 2
         sent = lax.dynamic_slice_in_dim(piece, (1 - bit) * half, half, 0)
         kept = lax.dynamic_slice_in_dim(piece, bit * half, half, 0)
-        piece = kept + lax.ppermute(sent, AXES, partners(step))
-    held = jnp.concatenate([piece, mean_rows], axis=0)[None]
-    for step in reversed(range(bits)):
-        other = lax.ppermute(held, AXES, partners(step))
-        if step:
-            held = jnp.concatenate([held, other], axis=0)
-    return held, other, jnp.stack([mine, twin])
+        to = [(d, d ^ (1 << orders[d & 1][step])) for d in range(devices)]
+        piece = kept + lax.ppermute(sent, AXES, to)
+    held = jnp.concatenate([piece, mean_rows], axis=0)
+    held = jnp.broadcast_to(held[None], (wide // 2,) + held.shape)
+    held = lax.all_to_all(held, "wide", 0, 0, axis_index_groups=same_core)
+    held = jnp.broadcast_to(held[None], (groups,) + held.shape)
+    held = lax.all_to_all(held, "grp", 0, 0)
+    held = held.reshape((-1,) + held.shape[2:])
+    other = lax.ppermute(held, "wide", twins)
+    even, odd = ([number(d) for d in range(c, devices, 2)] for c in range(2))
+    numbers = jnp.where(
+        core == 0, jnp.array(even + odd, jnp.int32), jnp.array(odd + even, jnp.int32)
+    )
+    return held, other, numbers
 
 
 def factor_block(block, upper_ref, inverse_ref):
@@ -237,7 +241,7 @@
     for part, ref in enumerate((held_ref, other_ref)):
 
         def unpack(q, _):
-            p = numbers_ref[part] ^ q
+            p = numbers_ref[part * half + q]
             to = pl.multiple_of(p * piece_rows, SUB)
             packed[pl.ds(to, piece_rows), :] = ref[q, :piece_rows, :]
             to = pl.multiple_of(p * SUB, SUB)

time: 98.8 us -> 98.3 us (level)
  blocking collectives: 0 us -> 24.3 us
  waiting for transfers between devices: 32.2 us -> 17.6 us
  starting transfers between devices: 20.7 us -> 10.7 us
    all_to_all x0 -> x2, blocking collectives: none -> 24.3 us  [the longest x1 12.3 us: sum_in_pieces(): held = lax.all_to_all(held, 'wide', 0, 0, axis_index_groups=same_core)]
    ppermute x10 -> x6, waiting for transfers between devices: 32.2 us -> 17.6 us  [the longest x5 15.3 us: sum_in_pieces(): piece = kept + lax.ppermute(sent, AXES, to)]
    ppermute x10 -> x6, starting transfers between devices: 20.7 us -> 10.7 us  [the longest x5 10.7 us: sum_in_pieces(): piece = kept + lax.ppermute(sent, AXES, to)]
    unnamed x7 -> x8, local copies, waits for them, and re-layouts: 2.37 us -> 2.35 us
  transfers between devices with their start and end apart: 10 -> 6, of which waited for: 10 -> 6; matrix products, arithmetic and copies ran while one was open for 0% -> 0% of each run, Pallas kernels for 0% -> 0%
where the time goes in v5:
time: 98.3 us; the launch traced here: 98 us
  Pallas kernels  41.8 us (43%)
  blocking collectives  24.3 us (25%)
  waiting for transfers between devices  17.6 us (18%)
  starting transfers between devices  10.7 us (11%)
  local copies, waits for them, and re-layouts  2.58 us (3%)
    pallas_call x1, Pallas kernels, factor_and_inverse(): pl.pallas_call(factor_kernel, out_shape=(jax.ShapeDtypeStruct((width, wid...  28.1 us
    ppermute x5, waiting for transfers between devices, sum_in_pieces(): piece = kept + lax.ppermute(sent, AXES, to)  15.3 us
    all_to_all x1, blocking collectives, sum_in_pieces(): held = lax.all_to_all(held, 'wide', 0, 0, axis_index_groups=same_core)  12.3 us
    all_to_all x1, blocking collectives, sum_in_pieces(): held = lax.all_to_all(held, 'grp', 0, 0)  12 us
    ppermute x5, starting transfers between devices, sum_in_pieces(): piece = kept + lax.ppermute(sent, AXES, to)  10.7 us
    pallas_call x1, Pallas kernels, whiten(): pl.pallas_call(whiten_kernel, grid=(rows // TILE,), out_shape=jax.ShapeDt...  8.29 us
    pallas_call x1, Pallas kernels, local_gram(): pl.pallas_call(gram_kernel, out_shape=(jax.ShapeDtypeStruct((packed_rows,...  5.41 us
    unnamed x8, local copies, waits for them, and re-layouts  2.35 us
  transfers between devices with their start and end apart: 6, of which 6 were waited for; matrix products, arithmetic and copies ran while one was open for 0% of the time, Pallas kernels for 0%

profile of v5, /device:TPU:0, one launch (start us, length us, event | category | flops | bytes accessed | tf_op | source)
XLA Modules:
  0.0 98.0 jit_solution(6217529652777594198)
XLA Ops:
  0.6 0.0 copy-start
  0.6 2.3 %copy-done = f32[1536,768]{1,0:T(8,128)S(1)} copy-done((f32[1536,768]{1,0:T(8,128)S(1)}, f32[1536,768]{1,0:T(8,128)}, u32[]{:S(2)}) %copy-start) | copy-done | bytes 4718616
  3.0 5.4 %shard_map.59 = (f32[2816,128]{1,0:T(8,128)S(1)}, f32[8,128]{1,0:T(8,128)S(1)}) custom-call(f32[1536,768]{1,0:T(8,128)S(1)} %copy-done), custom_call_target="tpu_custom_call" | custom-call | tf_op jit(solution)/shard_map/pallas_call | solution.py:81
  8.4 0.1 constant_dynamic-slice_fusion.4
  8.5 0.5 collective-permute-start
  9.0 1.8 %collective-permute-done = f32[1408,128]{1,0:T(8,128)S(1)} collective-permute-done((f32[1408,128]{1,0:T(8,128)S(1)}, f32[1408,128]{1,0:T(8,128)S(1)}, u32[]{:S(2)}, u32[]{:S(2)}) %collective-permute-start) | collective-permute-done | bytes 720928 | tf_op jit(solution)/shard_map/ppermute | solution.py:121
  10.8 0.1 dynamic-slice_add_fusion
  10.9 2.9 %collective-permute-start.1 = (f32[704,128]{1,0:T(8,128)S(1)}, f32[704,128]{1,0:T(8,128)S(1)}, u32[]{:S(2)}, u32[]{:S(2)}) collective-permute-start(f32[704,128]{1,0:T(8,128)S(1)} %constant_dynamic-slice_fusion.3), channel_id=1, source_target_pairs={{0,8},{1,17},{2,10},{3,19},{4,12},{5,21},{6,14},{7,23},{8,0},{9,25... | collective-permute-start | bytes 1081352 | tf_op jit(solution)/shard_map/ppermute | solution.py:121
  13.9 5.4 %collective-permute-done.1 = f32[704,128]{1,0:T(8,128)S(1)} collective-permute-done((f32[704,128]{1,0:T(8,128)S(1)}, f32[704,128]{1,0:T(8,128)S(1)}, u32[]{:S(2)}, u32[]{:S(2)}) %collective-permute-start.1) | collective-permute-done | bytes 360480 | tf_op jit(solution)/shard_map/ppermute | solution.py:121
  19.3 2.2 %collective-permute-start.2 = (f32[352,128]{1,0:T(8,128)S(1)}, f32[352,128]{1,0:T(8,128)S(1)}, u32[]{:S(2)}, u32[]{:S(2)}) collective-permute-start(f32[352,128]{1,0:T(8,128)S(1)} %constant_dynamic-slice_fusion.2), channel_id=1, source_target_pairs={{0,2},{1,9},{2,0},{3,11},{4,6},{5,13},{6,4},{7,15},{8,10},{9,1},{1... | collective-permute-start | bytes 540680 | tf_op jit(solution)/shard_map/ppermute | solution.py:121
  21.5 3.5 %collective-permute-done.2 = f32[352,128]{1,0:T(8,128)S(1)} collective-permute-done((f32[352,128]{1,0:T(8,128)S(1)}, f32[352,128]{1,0:T(8,128)S(1)}, u32[]{:S(2)}, u32[]{:S(2)}) %collective-permute-start.2) | collective-permute-done | bytes 180256 | tf_op jit(solution)/shard_map/ppermute | solution.py:121
  25.0 2.0 %collective-permute-start.3 = (f32[176,128]{1,0:T(8,128)S(1)}, f32[176,128]{1,0:T(8,128)S(1)}, u32[]{:S(2)}, u32[]{:S(2)}) collective-permute-start(f32[176,128]{1,0:T(8,128)S(1)} %constant_dynamic-slice_fusion.1), channel_id=1, source_target_pairs={{0,16},{1,3},{2,18},{3,1},{4,20},{5,7},{6,22},{7,5},{8,24},{9,11},... | collective-permute-start | bytes 270344 | tf_op jit(solution)/shard_map/ppermute | solution.py:121
  27.1 2.6 %collective-permute-done.3 = f32[176,128]{1,0:T(8,128)S(1)} collective-permute-done((f32[176,128]{1,0:T(8,128)S(1)}, f32[176,128]{1,0:T(8,128)S(1)}, u32[]{:S(2)}, u32[]{:S(2)}) %collective-permute-start.3) | collective-permute-done | bytes 90144 | tf_op jit(solution)/shard_map/ppermute | solution.py:121
  29.7 3.1 %collective-permute-start.4 = (f32[88,128]{1,0:T(8,128)S(1)}, f32[88,128]{1,0:T(8,128)S(1)}, u32[]{:S(2)}, u32[]{:S(2)}) collective-permute-start(f32[88,128]{1,0:T(8,128)S(1)} %constant_dynamic-slice_fusion), channel_id=1, source_target_pairs={{0,4},{1,5},{2,6},{3,7},{4,0},{5,1},{6,2},{7,3},{8,12},{9,13},{10,... | collective-permute-start | bytes 135176 | tf_op jit(solution)/shard_map/ppermute | solution.py:121
  32.8 2.0 %collective-permute-done.4 = f32[88,128]{1,0:T(8,128)S(1)} collective-permute-done((f32[88,128]{1,0:T(8,128)S(1)}, f32[88,128]{1,0:T(8,128)S(1)}, u32[]{:S(2)}, u32[]{:S(2)}) %collective-permute-start.4) | collective-permute-done | bytes 45088 | tf_op jit(solution)/shard_map/ppermute | solution.py:121
  34.8 0.0 copy-start.2
  34.9 0.0 copy-start.3
  34.9 0.0 copy-start.1
  34.9 12.3 %all_to_all.10 = f32[4,96,128]{2,1,0:T(8,128)S(1)} all-to-all(f32[4,96,128]{2,1,0:T(8,128)S(1)} %broadcast_in_dim.4), channel_id=1, replica_groups={{0,2,4,6},{1,3,5,7},{8,10,12,14},{9,11,13,15},{16,18,20,22},{17,19,21,2..., dimensions={0} | all-to-all | bytes 393216 | tf_op jit(solution)/shard_map/all_to_all | solution.py:124
  47.2 0.1 broadcast_in_dim.5
  47.3 12.0 %all_to_all.11 = f32[4,4,96,128]{3,2,1,0:T(8,128)S(1)} all-to-all(f32[4,4,96,128]{3,2,1,0:T(8,128)S(1)} %broadcast_in_dim.5), channel_id=1, replica_groups=mesh['grp'=4,'wide'=8] {'grp'}, dimensions={0} | all-to-all | bytes 1572864 | tf_op jit(solution)/shard_map/all_to_all | solution.py:126
  59.3 0.0 collective-permute-start.5
  59.3 0.0 copy-done.2
  59.3 0.0 copy-done.3
  59.3 2.3 %collective-permute-done.5.other_ref = f32[16,96,128]{2,1,0:T(8,128)S(1)} collective-permute-done((f32[16,96,128]{2,1,0:T(8,128)S(1)}, f32[16,96,128]{2,1,0:T(8,128)S(1)}, u32[]{:S(2)}, u32[]{:S(2)}) %collective-permute-start.5) | collective-permute-done | bytes 786464 | tf_op jit(solution)/shard_map/ppermute | solution.py:128
  61.6 0.0 copy-done.1
  61.6 28.1 %shard_map.60 = (f32[768,768]{1,0:T(8,128)}, bf16[768,768]{1,0:T(8,128)(2,1)S(1)}, bf16[768,768]{1,0:T(8,128)(2,1)S(1)}, f32[8,768]{1,0:T(8,128)S(1)}) custom-call(f32[16,96,128]{2,1,0:T(8,128)S(1)} %bitcast.2, f32[16,96,128]{2,1,0:T(8,128)S(1)} %collective-permute-done.5.other_ref, s32[32]{0:T(128)S(1)} %broadcast_select_fusion.numbers_ref, f32[2]{0:T(128)S(1)} %copy-done.1), custom_call_target="tpu_custom_call" | custom-call | tf_op jit(solution)/shard_map/pallas_call | solution.py:365
  89.7 8.3 %shard_map.61 = f32[1536,768]{1,0:T(8,128)} custom-call(f32[1536,768]{1,0:T(8,128)} %x_ref.3, f32[8,768]{1,0:T(8,128)S(1)} %get-tuple-element.10.mean_ref, bf16[768,768]{1,0:T(8,128)(2,1)S(1)} %get-tuple-element.11.high_ref, bf16[768,768]{1,0:T(8,128)(2,1)S(1)} %get-tuple-element.12.low_ref), custom_call_target="tpu_custom_call" | custom-call | tf_op jit(solution)/shard_map/pallas_call | solution.py:400
  (11 shorter events, 0.2 us)
Async XLA Ops:
  0.6 2.3 %copy-start = (f32[1536,768]{1,0:T(8,128)S(1)}, f32[1536,768]{1,0:T(8,128)}, u32[]{:S(2)}) copy-start(f32[1536,768]{1,0:T(8,128)} %x_ref.3) | copy-start | bytes 14155780
  8.5 2.3 %collective-permute-start = (f32[1408,128]{1,0:T(8,128)S(1)}, f32[1408,128]{1,0:T(8,128)S(1)}, u32[]{:S(2)}, u32[]{:S(2)}) collective-permute-start(f32[1408,128]{1,0:T(8,128)S(1)} %constant_dynamic-slice_fusion.4), channel_id=1, source_target_pairs={{0,1},{1,0},{2,3},{3,2},{4,5},{5,4},{6,7},{7,6},{8,9},{9,8},{10,11... | collective-permute-start | bytes 2162696 | tf_op jit(solution)/shard_map/ppermute | solution.py:121
  10.9 8.3 %collective-permute-start.1 = (f32[704,128]{1,0:T(8,128)S(1)}, f32[704,128]{1,0:T(8,128)S(1)}, u32[]{:S(2)}, u32[]{:S(2)}) collective-permute-start(f32[704,128]{1,0:T(8,128)S(1)} %constant_dynamic-slice_fusion.3), channel_id=1, source_target_pairs={{0,8},{1,17},{2,10},{3,19},{4,12},{5,21},{6,14},{7,23},{8,0},{9,25... | collective-permute-start | bytes 1081352 | tf_op jit(solution)/shard_map/ppermute | solution.py:121
  19.3 5.6 %collective-permute-start.2 = (f32[352,128]{1,0:T(8,128)S(1)}, f32[352,128]{1,0:T(8,128)S(1)}, u32[]{:S(2)}, u32[]{:S(2)}) collective-permute-start(f32[352,128]{1,0:T(8,128)S(1)} %constant_dynamic-slice_fusion.2), channel_id=1, source_target_pairs={{0,2},{1,9},{2,0},{3,11},{4,6},{5,13},{6,4},{7,15},{8,10},{9,1},{1... | collective-permute-start | bytes 540680 | tf_op jit(solution)/shard_map/ppermute | solution.py:121
  25.0 4.6 %collective-permute-start.3 = (f32[176,128]{1,0:T(8,128)S(1)}, f32[176,128]{1,0:T(8,128)S(1)}, u32[]{:S(2)}, u32[]{:S(2)}) collective-permute-start(f32[176,128]{1,0:T(8,128)S(1)} %constant_dynamic-slice_fusion.1), channel_id=1, source_target_pairs={{0,16},{1,3},{2,18},{3,1},{4,20},{5,7},{6,22},{7,5},{8,24},{9,11},... | collective-permute-start | bytes 270344 | tf_op jit(solution)/shard_map/ppermute | solution.py:121
  29.7 5.1 %collective-permute-start.4 = (f32[88,128]{1,0:T(8,128)S(1)}, f32[88,128]{1,0:T(8,128)S(1)}, u32[]{:S(2)}, u32[]{:S(2)}) collective-permute-start(f32[88,128]{1,0:T(8,128)S(1)} %constant_dynamic-slice_fusion), channel_id=1, source_target_pairs={{0,4},{1,5},{2,6},{3,7},{4,0},{5,1},{6,2},{7,3},{8,12},{9,13},{10,... | collective-permute-start | bytes 135176 | tf_op jit(solution)/shard_map/ppermute | solution.py:121
  34.8 24.5 %copy-start.2 = (s32[32]{0:T(128)S(1)}, s32[32]{0:T(128)}, u32[]{:S(2)}) copy-start(s32[32]{0:T(128)} %constant.39.clone) | copy-start | bytes 388
  34.9 24.5 %copy-start.3 = (s32[32]{0:T(128)S(1)}, s32[32]{0:T(128)}, u32[]{:S(2)}) copy-start(s32[32]{0:T(128)} %constant.38.clone) | copy-start | bytes 388
  34.9 26.7 %copy-start.1 = (f32[2]{0:T(128)S(1)}, f32[2]{0:T(128)}, u32[]{:S(2)}) copy-start(f32[2]{0:T(128)} %constant.40.clone.count_ref) | copy-start | bytes 28
  59.3 2.3 %collective-permute-start.5 = (f32[16,96,128]{2,1,0:T(8,128)S(1)}, f32[16,96,128]{2,1,0:T(8,128)S(1)}, u32[]{:S(2)}, u32[]{:S(2)}) collective-permute-start(f32[16,96,128]{2,1,0:T(8,128)S(1)} %bitcast.1), channel_id=1, source_target_pairs={{0,1},{1,0},{2,3},{3,2},{4,5},{5,4},{6,7},{7,6},{8,9},{9,8},{10,11... | collective-permute-start | bytes 2359304 | tf_op jit(solution)/shard_map/ppermute | solution.py:128

commit v6 on v4

--- a/solution.py
+++ b/solution.py
@@ -40,10 +40,24 @@
     return [(i, j) for i in range(n) for j in range(i, n)]
 
 
-def gram_kernel(x_ref, packed_ref, mean_ref, both_ref, swapped_ref):
+def chunk_copies(source, target, arrived):
+    return [
+        pltpu.make_async_copy(
+            source.at[pl.ds(r, TILE), :], target.at[pl.ds(r, TILE), :], arrived.at[r // TILE]
+        )
+        for r in range(0, source.shape[0], TILE)
+    ]
+
+
+def gram_kernel(x_hbm, packed_ref, mean_ref, x_ref, both_ref, swapped_ref, arrived):
     rows, width = x_ref.shape
+    copies = chunk_copies(x_hbm, x_ref, arrived)
+    for copy in copies:
+        copy.start()
     total = jnp.zeros((SUB, width), jnp.float32)
     for r in range(0, rows, LANES):
+        if r % TILE == 0:
+            copies[r // TILE].wait()
         part = x_ref[r : r + LANES, :]
         for q in range(0, LANES, SUB):
             total = total + part[q : q + SUB, :]
@@ -84,9 +98,11 @@
             jax.ShapeDtypeStruct((packed_rows, LANES), jnp.float32),
             jax.ShapeDtypeStruct((mean_rows, LANES), jnp.float32),
         ),
-        in_specs=[pl.BlockSpec(memory_space=pltpu.VMEM)],
+        in_specs=[pl.BlockSpec(memory_space=pl.ANY)],
         out_specs=(pl.BlockSpec(memory_space=pltpu.VMEM),) * 2,
-        scratch_shapes=[pltpu.VMEM((2 * rows, width), jnp.bfloat16)] * 2,
+        scratch_shapes=[pltpu.VMEM((rows, width), jnp.float32)]
+        + [pltpu.VMEM((2 * rows, width), jnp.bfloat16)] * 2
+        + [pltpu.SemaphoreType.DMA((rows // TILE,))],
         compiler_params=pltpu.CompilerParams(vmem_limit_bytes=48 * 2**20),
     )(embeddings)
 
@@ -206,20 +222,30 @@
 
 
 def factor_kernel(
+    x_hbm,
     held_ref,
     other_ref,
     numbers_ref,
     count_ref,
+    out_hbm,
     factor_ref,
-    high_ref,
-    low_ref,
-    mean_ref,
     work,
     packed,
     means_scr,
     upper_ref,
     inverse_ref,
+    x_ref,
+    x_high,
+    x_low,
+    high_ref,
+    low_ref,
+    out_ref,
+    arrived,
+    left_for_out,
 ):
+    rows_in = chunk_copies(x_hbm, x_ref, arrived)
+    for copy in rows_in:
+        copy.start()
     half = held_ref.shape[0]
     pieces = 2 * half
     width = factor_ref.shape[0]
@@ -242,10 +268,7 @@
     middle = jnp.mean(stacked, axis=0)
     apart = stacked - middle[None]
     wide = jnp.concatenate([apart[:, b, :] for b in range(blocks)], axis=1)
-    for b in range(blocks):
-        mean_ref[:, LANES * b : LANES * (b + 1)] = jnp.broadcast_to(
-            middle[b : b + 1, :], (SUB, LANES)
-        )
+    col_mean = jnp.concatenate([middle[b : b + 1, :] for b in range(blocks)], axis=1)
     total_scale = count_ref[1]
     place = {block: LANES * p for p, block in enumerate(upper_blocks(width))}
     span = lambda b, e=None: slice(LANES * b, LANES * (b + 1 if e is None else e))
@@ -271,9 +294,32 @@
                 factor = jnp.where(col_at >= row_at, upper_ref[k % 2], 0.0)
                 back = inverse_ref[k % 2]
             factor_ref[span(k), span(j)] = factor * (1.0 / total_scale)
-            high, low = split(back * total_scale)
-            high_ref[span(k), span(j)] = high
-            low_ref[span(k), span(j)] = low
+            high, low = split((back * total_scale).T)
+            high_ref[span(j), span(k)] = high
+            low_ref[span(j), span(k)] = low
+
+    def centre(chunk):
+        here = slice(TILE * chunk, TILE * (chunk + 1))
+        rows_in[chunk].wait()
+        high, low = split(x_ref[here, :] - col_mean)
+        x_high[here, :] = high
+        x_low[here, :] = low
+
+    rows_out = []
+
+    def whiten(chunk, right):
+        here = slice(TILE * chunk, TILE * (chunk + 1))
+        cols, deep = slice(right, right + TILE), slice(0, right + TILE)
+        tile = fast_dot(x_low[here, deep], high_ref[deep, cols], ((1,), (0,)))
+        tile = tile + fast_dot(x_high[here, deep], low_ref[deep, cols], ((1,), (0,)))
+        out_ref[here, cols] = tile + fast_dot(
+            x_high[here, deep], high_ref[deep, cols], ((1,), (0,))
+        )
+        copy = pltpu.make_async_copy(
+            out_ref.at[here, cols], out_hbm.at[here, cols], left_for_out.at[len(rows_out)]
+        )
+        copy.start()
+        rows_out.append(copy)
 
     def below(k, i, left, right, first):
         change = parts_dot(left, [r[:, : LANES * (k + 1)] for r in right])
@@ -322,6 +368,8 @@
     gather(0, 0, 1)
     todo = [lambda: gather(0, 1, blocks)]
     todo += [lambda i=i: gather(i, i, blocks) for i in range(1, blocks)]
+    todo += [lambda c=c: centre(c) for c in range(len(rows_in))]
+    waiting = []
     for k in range(blocks):
         groups = LANES // SUB
         done = 0
@@ -339,78 +387,62 @@
             work[span(k + 1), span(k + 1)] = work[span(k + 1), span(k + 1)] - parts_dot(
                 turned, right_parts(solved)
             )
-        todo = later(k, left, solved, turned)
+        todo = later(k, left, solved, turned) + waiting
+        waiting = []
+        if LANES * (k + 1) % TILE == 0:
+            right = LANES * (k + 1) - TILE
+            white = [lambda c=c, r=right: whiten(c, r) for c in range(len(rows_in))]
+            share = len(white) if k + 1 == blocks else len(white) // 2
+            todo, waiting = todo + white[:share], white[share:]
     for piece in todo:
         piece()
-
-
-def factor_and_inverse(held, other, numbers, piece_rows, width, local_rows):
+    for copy in rows_out:
+        copy.wait()
+
+
+def factor_and_whiten(embeddings, held, other, numbers, piece_rows):
+    rows, width = embeddings.shape
     pieces = 2 * held.shape[0]
     vmem = pl.BlockSpec(memory_space=pltpu.VMEM)
     smem = pl.BlockSpec(memory_space=pltpu.SMEM)
-    half_type = jax.ShapeDtypeStruct((width, width), jnp.bfloat16)
-    counts = jnp.array([local_rows, (local_rows * pieces) ** 0.5], jnp.float32)
+    anywhere = pl.BlockSpec(memory_space=pl.ANY)
+    chunks = rows // TILE
+    counts = jnp.array([rows, (rows * pieces) ** 0.5], jnp.float32)
     return pl.pallas_call(
         factor_kernel,
         out_shape=(
+            jax.ShapeDtypeStruct((rows, width), jnp.float32),
             jax.ShapeDtypeStruct((width, width), jnp.float32),
-            half_type,
-            half_type,
-            jax.ShapeDtypeStruct((SUB, width), jnp.float32),
         ),
-        in_specs=[vmem, vmem, smem, smem],
-        out_specs=(vmem,) * 4,
+        in_specs=[anywhere, vmem, vmem, smem, smem],
+        out_specs=(anywhere, vmem),
         scratch_shapes=[
             pltpu.VMEM((width, width), jnp.float32),
             pltpu.VMEM((pieces * piece_rows, LANES), jnp.float32),
             pltpu.VMEM((pieces * SUB, LANES), jnp.float32),
             pltpu.VMEM((2, LANES, LANES), jnp.float32),
             pltpu.VMEM((2, LANES, LANES), jnp.float32),
+            pltpu.VMEM((rows, width), jnp.float32),
+            pltpu.VMEM((rows, width), jnp.bfloat16),
+            pltpu.VMEM((rows, width), jnp.bfloat16),
+            pltpu.VMEM((width, width), jnp.bfloat16),
+            pltpu.VMEM((width, width), jnp.bfloat16),
+            pltpu.VMEM((rows, width), jnp.float32),
+            pltpu.SemaphoreType.DMA((chunks,)),
+            pltpu.SemaphoreType.DMA((chunks * (width // TILE),)),
         ],
         compiler_params=pltpu.CompilerParams(vmem_limit_bytes=48 * 2**20),
-    )(held, other, numbers, counts)
-
-
-def whiten_kernel(x_ref, mean_ref, high_ref, low_ref, out_ref):
-    width = x_ref.shape[1]
-    high, low = split(x_ref[...] - mean_ref[:1, :])
-    for right in range(0, width, TILE):
-        here = slice(right, right + TILE)
-        deep = slice(0, right + TILE)
-        tile = fast_dot(high[:, deep], high_ref[here, deep], ((1,), (1,)))
-        tile = tile + fast_dot(high[:, deep], low_ref[here, deep], ((1,), (1,)))
-        out_ref[:, here] = tile + fast_dot(low[:, deep], high_ref[here, deep], ((1,), (1,)))
-
-
-def whiten(embeddings, mean, high, low):
-    rows, width = embeddings.shape
-    whole = lambda i: (0, 0)
-    return pl.pallas_call(
-        whiten_kernel,
-        grid=(rows // TILE,),
-        out_shape=jax.ShapeDtypeStruct((rows, width), jnp.float32),
-        in_specs=[
-            pl.BlockSpec((TILE, width), lambda i: (i, 0)),
-            pl.BlockSpec(mean.shape, whole),
-            pl.BlockSpec((width, width), whole),
-            pl.BlockSpec((width, width), whole),
-        ],
-        out_specs=pl.BlockSpec((TILE, width), lambda i: (i, 0)),
-        compiler_params=pltpu.CompilerParams(vmem_limit_bytes=48 * 2**20),
-    )(embeddings, mean, high, low)
+    )(embeddings, held, other, numbers, counts)
 
 
 def shards(embeddings):
-    local_rows, width = embeddings.shape
+    _, width = embeddings.shape
     devices = lax.axis_size("grp") * lax.axis_size("wide")
     used = LANES * len(upper_blocks(width))
     piece_rows = -(-used // (SUB * devices)) * SUB
     packed, mean_rows = local_gram(embeddings, piece_rows * devices, SUB)
     held, other, numbers = sum_in_pieces(packed, mean_rows)
-    factor, high, low, mean = factor_and_inverse(
-        held, other, numbers, piece_rows, width, local_rows
-    )
-    return (whiten(embeddings, mean, high, low), factor)
+    return factor_and_whiten(embeddings, held, other, numbers, piece_rows)
 
 
 def solution(mesh):

time: 97.7 us -> 96.7 us (0.990)
  Pallas kernels: 41.8 us -> 40.7 us
    pallas_call x2 -> x1, Pallas kernels: 36.4 us -> 34.9 us  [factor_and_whiten(): pl.pallas_call(factor_kernel, out_shape=(jax.ShapeDtypeStruct((rows, widt...]
where the time goes in v6:
time: 96.7 us; the launch traced here: 96.4 us
  blocking collectives  47.5 us (49%)
  Pallas kernels  40.7 us (42%)
  waiting for transfers between devices  4.03 us (4%)
  local copies, waits for them, and re-layouts  2.48 us (3%)
    pallas_call x1, Pallas kernels, factor_and_whiten(): pl.pallas_call(factor_kernel, out_shape=(jax.ShapeDtypeStruct((rows, widt...  34.9 us
    all_to_all x2, blocking collectives, over_grp(): return lax.all_to_all(parts, 'grp', 0, 0)  26.9 us
    all_to_all x2, blocking collectives, over_wide(): return lax.all_to_all(parts, 'wide', 0, 0, axis_index_groups=same_core)  20.6 us
    pallas_call x1, Pallas kernels, local_gram(): pl.pallas_call(gram_kernel, out_shape=(jax.ShapeDtypeStruct((packed_rows,...  5.8 us
    unnamed x4, local copies, waits for them, and re-layouts  2.34 us
    ppermute x1, waiting for transfers between devices, sum_in_pieces(): other = lax.ppermute(held, 'wide', twins)  2.21 us
  transfers between devices with their start and end apart: 2, of which 2 were waited for; matrix products, arithmetic and copies ran while one was open for 0% of the time, Pallas kernels for 0%

profile of v6, /device:TPU:0, one launch (start us, length us, event | category | flops | bytes accessed | tf_op | source)
XLA Modules:
  0.0 96.4 jit_solution(9325029431000348740)
XLA Ops:
  0.6 0.0 copy-start
  0.6 2.3 %copy-done = f32[1536,768]{1,0:T(8,128)S(1)} copy-done((f32[1536,768]{1,0:T(8,128)S(1)}, f32[1536,768]{1,0:T(8,128)}, u32[]{:S(2)}) %copy-start) | copy-done | bytes 4718616
  3.0 5.8 %shard_map.41 = (f32[2816,128]{1,0:T(8,128)S(1)}, f32[8,128]{1,0:T(8,128)S(1)}) custom-call(f32[1536,768]{1,0:T(8,128)S(1)} %copy-done), custom_call_target="tpu_custom_call" | custom-call | tf_op jit(solution)/shard_map/pallas_call | solution.py:95
  8.8 0.1 constant_dynamic-slice_fusion
  8.8 0.5 collective-permute-start
  9.4 1.8 %collective-permute-done = f32[1408,128]{1,0:T(8,128)S(1)} collective-permute-done((f32[1408,128]{1,0:T(8,128)S(1)}, f32[1408,128]{1,0:T(8,128)S(1)}, u32[]{:S(2)}, u32[]{:S(2)}) %collective-permute-start) | collective-permute-done | bytes 720928 | tf_op jit(solution)/shard_map/ppermute | solution.py:128
  11.2 0.1 dynamic-slice_add_fusion
  11.3 16.0 %all_to_all.20 = f32[4,352,128]{2,1,0:T(8,128)S(1)} all-to-all(f32[4,352,128]{2,1,0:T(8,128)S(1)} %bitcast.7), channel_id=1, replica_groups=mesh['grp'=4,'wide'=8] {'grp'}, dimensions={0} | all-to-all | bytes 1441792 | tf_op jit(solution)/shard_map/all_to_all | solution.py:117
  27.3 0.0 copy-start.1
  27.3 11.4 %all_to_all.21 = f32[4,88,128]{2,1,0:T(8,128)S(1)} all-to-all(f32[4,88,128]{2,1,0:T(8,128)S(1)} %bitcast.8), channel_id=1, replica_groups={{0,2,4,6},{1,3,5,7},{8,10,12,14},{9,11,13,15},{16,18,20,22},{17,19,21,2..., dimensions={0} | all-to-all | bytes 360448 | tf_op jit(solution)/shard_map/all_to_all | solution.py:120
  38.8 9.2 %all_to_all.22 = f32[4,96,128]{2,1,0:T(8,128)S(1)} all-to-all(f32[4,96,128]{2,1,0:T(8,128)S(1)} %broadcast_in_dim.4), channel_id=1, replica_groups={{0,2,4,6},{1,3,5,7},{8,10,12,14},{9,11,13,15},{16,18,20,22},{17,19,21,2..., dimensions={0} | all-to-all | bytes 393216 | tf_op jit(solution)/shard_map/all_to_all | solution.py:120
  48.0 0.1 broadcast_in_dim.5
  48.0 10.9 %all_to_all.23 = f32[4,4,96,128]{3,2,1,0:T(8,128)S(1)} all-to-all(f32[4,4,96,128]{3,2,1,0:T(8,128)S(1)} %broadcast_in_dim.5), channel_id=1, replica_groups=mesh['grp'=4,'wide'=8] {'grp'}, dimensions={0} | all-to-all | bytes 1572864 | tf_op jit(solution)/shard_map/all_to_all | solution.py:117
  59.0 0.0 collective-permute-start.1
  59.0 0.1 pad_add_fusion.numbers_ref
  59.1 2.2 %collective-permute-done.1.other_ref = f32[16,96,128]{2,1,0:T(8,128)S(1)} collective-permute-done((f32[16,96,128]{2,1,0:T(8,128)S(1)}, f32[16,96,128]{2,1,0:T(8,128)S(1)}, u32[]{:S(2)}, u32[]{:S(2)}) %collective-permute-start.1) | collective-permute-done | bytes 786464 | tf_op jit(solution)/shard_map/ppermute | solution.py:135
  61.3 0.0 copy-done.1
  61.3 34.9 %shard_map.42 = (f32[1536,768]{1,0:T(8,128)}, f32[768,768]{1,0:T(8,128)}) custom-call(f32[1536,768]{1,0:T(8,128)} %x_hbm.3, f32[16,96,128]{2,1,0:T(8,128)S(1)} %bitcast.6, f32[16,96,128]{2,1,0:T(8,128)S(1)} %collective-permute-done.1.other_ref, s32[2]{0:T(128)S(1)} %pad_add_fusion.numbers_ref, f32[2]{0:T(128)S(1)} %copy-done.1), custom_call_target="tpu_custom_call" | custom-call | tf_op jit(solution)/shard_map/pallas_call | solution.py:411
  (4 shorter events, 0.1 us)
Async XLA Ops:
  0.6 2.3 %copy-start = (f32[1536,768]{1,0:T(8,128)S(1)}, f32[1536,768]{1,0:T(8,128)}, u32[]{:S(2)}) copy-start(f32[1536,768]{1,0:T(8,128)} %x_hbm.3) | copy-start | bytes 14155780
  8.8 2.3 %collective-permute-start = (f32[1408,128]{1,0:T(8,128)S(1)}, f32[1408,128]{1,0:T(8,128)S(1)}, u32[]{:S(2)}, u32[]{:S(2)}) collective-permute-start(f32[1408,128]{1,0:T(8,128)S(1)} %constant_dynamic-slice_fusion), channel_id=1, source_target_pairs={{0,1},{1,0},{2,3},{3,2},{4,5},{5,4},{6,7},{7,6},{8,9},{9,8},{10,11... | collective-permute-start | bytes 2162696 | tf_op jit(solution)/shard_map/ppermute | solution.py:128
  27.3 34.0 %copy-start.1 = (f32[2]{0:T(128)S(1)}, f32[2]{0:T(128)}, u32[]{:S(2)}) copy-start(f32[2]{0:T(128)} %constant.18.clone.count_ref) | copy-start | bytes 28
  59.0 2.3 %collective-permute-start.1 = (f32[16,96,128]{2,1,0:T(8,128)S(1)}, f32[16,96,128]{2,1,0:T(8,128)S(1)}, u32[]{:S(2)}, u32[]{:S(2)}) collective-permute-start(f32[16,96,128]{2,1,0:T(8,128)S(1)} %bitcast.5), channel_id=1, source_target_pairs={{0,1},{1,0},{2,3},{3,2},{4,5},{5,4},{6,7},{7,6},{8,9},{9,8},{10,11... | collective-permute-start | bytes 2359304 | tf_op jit(solution)/shard_map/ppermute | solution.py:135

commit v7 on v6

--- a/solution.py
+++ b/solution.py
@@ -49,7 +49,7 @@
     ]
 
 
-def gram_kernel(x_hbm, packed_ref, mean_ref, x_ref, both_ref, swapped_ref, arrived):
+def gram_kernel(x_hbm, packed_ref, mean_ref, x_ref, split_ref, arrived):
     rows, width = x_ref.shape
     copies = chunk_copies(x_hbm, x_ref, arrived)
     for copy in copies:
@@ -64,17 +64,15 @@
     mean = jnp.sum(total, axis=0, keepdims=True) * (1.0 / rows)
     for r in range(0, rows, LANES):
         high, low = split(x_ref[r : r + LANES, :] - mean)
-        both_ref[r : r + LANES, :] = high
-        both_ref[rows + r : rows + r + LANES, :] = low
-        swapped_ref[r : r + LANES, :] = low
-        swapped_ref[rows + r : rows + r + LANES, :] = high
+        for part, value in enumerate((high, low, low, high)):
+            split_ref[rows * part + r : rows * part + r + LANES, :] = value
     place = {block: LANES * p for p, block in enumerate(upper_blocks(width))}
     for left in range(0, width, TILE):
-        turned = both_ref[:, left : left + TILE].T
+        turned = split_ref[: 2 * rows, left : left + TILE].T
+        turned = jnp.concatenate([turned, turned], axis=1)
         for right in range(left, width, TILE):
             here = slice(right, right + TILE)
-            tile = fast_dot(turned, both_ref[:, here], ((1,), (0,)))
-            tile = tile + fast_dot(turned, swapped_ref[:, here], ((1,), (0,)))
+            tile = fast_dot(turned, split_ref[:, here], ((1,), (0,)))
             for a in range(0, TILE, LANES):
                 for b in range(0, TILE, LANES):
                     block = ((left + a) // LANES, (right + b) // LANES)
@@ -101,9 +99,9 @@
         in_specs=[pl.BlockSpec(memory_space=pl.ANY)],
         out_specs=(pl.BlockSpec(memory_space=pltpu.VMEM),) * 2,
         scratch_shapes=[pltpu.VMEM((rows, width), jnp.float32)]
-        + [pltpu.VMEM((2 * rows, width), jnp.bfloat16)] * 2
+        + [pltpu.VMEM((4 * rows, width), jnp.bfloat16)]
         + [pltpu.SemaphoreType.DMA((rows // TILE,))],
-        compiler_params=pltpu.CompilerParams(vmem_limit_bytes=48 * 2**20),
+        compiler_params=pltpu.CompilerParams(vmem_limit_bytes=60 * 2**20),
     )(embeddings)
 
 
@@ -140,56 +138,57 @@
 def factor_block(block, upper_ref, inverse_ref):
     groups = LANES // SUB
     tiles = [block[SUB * p : SUB * (p + 1), :] for p in range(groups)]
-    row_at = lax.broadcasted_iota(jnp.int32, (SUB, LANES), 0)
     lane_at = lax.broadcasted_iota(jnp.int32, (SUB, LANES), 1)
-    unit = [
-        jnp.where(lane_at == row_at + SUB * p, 1.0, 0.0).astype(jnp.float32)
-        for p in range(groups)
-    ]
     for g in range(groups):
         base = SUB * g
         ahead = g + 1 < groups
+        own = (lane_at >= base) & (lane_at < base + SUB)
+        at_lane = [lane_at == base + i for i in range(SUB)]
         rows = [over_rows(tiles[g], i) for i in range(SUB)]
         s = {
             (i, j): over_lanes(rows[i], base + j) for i in range(SUB) for j in range(i, SUB)
         }
-        carried = [over_rows(unit[g], i) for i in range(SUB)]
+        rows = [
+            jnp.where(own, jnp.where(at_lane[i], 1.0, 0.0), rows[i]) for i in range(SUB)
+        ]
         if ahead:
             column = [over_lanes(tiles[g + 1], base + i) for i in range(SUB)]
+            tiles[g + 1] = jnp.where(own, 0.0, tiles[g + 1])
         scale = []
         for j in range(SUB):
             r = lax.rsqrt(s[j, j])
             scale.append(r)
-            for k in range(j + 1, SUB):
+            for k in range(j, SUB):
                 s[j, k] = s[j, k] * r
             for k in range(j + 1, SUB):
                 for m in range(k, SUB):
                     s[k, m] = s[k, m] - s[j, k] * s[j, m]
             rows[j] = rows[j] * r
-            carried[j] = carried[j] * r
             for k in range(j + 1, SUB):
                 rows[k] = rows[k] - s[j, k] * rows[j]
-                carried[k] = carried[k] - s[j, k] * carried[j]
             if ahead:
                 column[j] = column[j] * r
                 for k in range(j + 1, SUB):
                     column[k] = column[k] - column[j] * s[j, k]
                 tiles[g + 1] = tiles[g + 1] - column[j] * rows[j]
-                unit[g + 1] = unit[g + 1] - column[j] * carried[j]
-            upper_ref[base + j : base + j + 1, :] = rows[j][:1, :]
-            inverse_ref[base + j : base + j + 1, :] = carried[j][:1, :]
+            inverse_ref[base + j : base + j + 1, :] = rows[j][:1, :]
+            upper = rows[j]
+            for k in range(j, SUB):
+                upper = jnp.where(at_lane[k], s[j, k], upper)
+            upper_ref[base + j : base + j + 1, :] = upper[:1, :]
         if g + 2 < groups:
             for i in reversed(range(SUB)):
                 for k in range(i + 1, SUB):
                     rows[i] = rows[i] - s[i, k] * rows[k]
-                    carried[i] = carried[i] - s[i, k] * carried[k]
                 rows[i] = rows[i] * scale[i]
-                carried[i] = carried[i] * scale[i]
         for p in range(g + 2, groups):
             column = [over_lanes(tiles[p], base + i) for i in range(SUB)]
-            tiles[p] = tiles[p] - tree_sum([c * x for c, x in zip(column, rows)])
-            unit[p] = unit[p] - tree_sum([c * x for c, x in zip(column, carried)])
+            change = tree_sum([c * x for c, x in zip(column, rows)])
+            tiles[p] = jnp.where(own, 0.0, tiles[p]) - change
         yield
+    row_group = lax.broadcasted_iota(jnp.int32, (LANES, LANES), 0) // SUB
+    lane_group = lax.broadcasted_iota(jnp.int32, (LANES, LANES), 1) // SUB
+    inverse_ref[...] = jnp.where(lane_group <= row_group, inverse_ref[...], 0.0)
 
 
 def tree_sum(terms):
@@ -207,18 +206,16 @@
 
 def left_parts(values):
     high, middle, low = in_three(values)
-    return jnp.concatenate([high, middle], axis=1), jnp.concatenate([low, high], axis=1)
+    return jnp.concatenate([high, middle, high, middle, high, low], axis=1)
 
 
 def right_parts(values):
     high, middle, low = in_three(values)
-    stack = lambda a, b: jnp.concatenate([a, b], axis=0)
-    return stack(high, high), stack(middle, middle), stack(high, low)
+    return jnp.concatenate([high, high, middle, middle, low, high], axis=0)
 
 
 def parts_dot(left, right):
-    plain = lambda a, b: fast_dot(a, b, ((1,), (0,)))
-    return (plain(left[1], right[2]) + plain(left[0], right[1])) + plain(left[0], right[0])
+    return fast_dot(left, right, ((1,), (0,)))
 
 
 def factor_kernel(
@@ -300,37 +297,41 @@
 
     def centre(chunk):
         here = slice(TILE * chunk, TILE * (chunk + 1))
-        rows_in[chunk].wait()
         high, low = split(x_ref[here, :] - col_mean)
         x_high[here, :] = high
         x_low[here, :] = low
 
     rows_out = []
+    whitened = []
 
     def whiten(chunk, right):
         here = slice(TILE * chunk, TILE * (chunk + 1))
         cols, deep = slice(right, right + TILE), slice(0, right + TILE)
-        tile = fast_dot(x_low[here, deep], high_ref[deep, cols], ((1,), (0,)))
-        tile = tile + fast_dot(x_high[here, deep], low_ref[deep, cols], ((1,), (0,)))
-        out_ref[here, cols] = tile + fast_dot(
-            x_high[here, deep], high_ref[deep, cols], ((1,), (0,))
+        high, low = x_high[here, deep], x_low[here, deep]
+        back_high, back_low = high_ref[deep, cols], low_ref[deep, cols]
+        out_ref[here, cols] = fast_dot(
+            jnp.concatenate([high, high, low], axis=1),
+            jnp.concatenate([back_high, back_low, back_high], axis=0),
+            ((1,), (0,)),
         )
-        copy = pltpu.make_async_copy(
-            out_ref.at[here, cols], out_hbm.at[here, cols], left_for_out.at[len(rows_out)]
-        )
-        copy.start()
-        rows_out.append(copy)
+        whitened.append((here, cols))
+
+    def send_whitened():
+        for here, cols in whitened[len(rows_out) :]:
+            copy = pltpu.make_async_copy(
+                out_ref.at[here, cols], out_hbm.at[here, cols], left_for_out.at[len(rows_out)]
+            )
+            copy.start()
+            rows_out.append(copy)
 
     def below(k, i, left, right, first):
-        change = parts_dot(left, [r[:, : LANES * (k + 1)] for r in right])
+        change = parts_dot(left, right[:, : LANES * (k + 1)])
         if k:
             work[span(i), span(0, k)] = work[span(i), span(0, k)] - change[:, : LANES * k]
         work[span(i), span(k)] = -change[:, LANES * k :]
         if first < blocks:
             cols = span(first, blocks)
-            work[span(i), cols] = work[span(i), cols] - parts_dot(
-                left, [r[:, cols] for r in right]
-            )
+            work[span(i), cols] = work[span(i), cols] - parts_dot(left, right[:, cols])
 
     def later(k, left, solved, turned):
         row = {}
@@ -368,17 +369,21 @@
     gather(0, 0, 1)
     todo = [lambda: gather(0, 1, blocks)]
     todo += [lambda i=i: gather(i, i, blocks) for i in range(1, blocks)]
-    todo += [lambda c=c: centre(c) for c in range(len(rows_in))]
     waiting = []
     for k in range(blocks):
         groups = LANES // SUB
         done = 0
+        if k == 1:
+            for copy in rows_in:
+                copy.wait()
+            todo += [lambda c=c: centre(c) for c in range(len(rows_in))]
         steps = factor_block(work[span(k), span(k)], upper_ref.at[k % 2], inverse_ref.at[k % 2])
         for g, _ in enumerate(steps):
             due = -(-len(todo) * (g + 1) // groups)
             for piece in todo[done:due]:
                 piece()
             done = due
+        send_whitened()
         left = left_parts(inverse_ref[k % 2])
         solved = turned = None
         if k + 1 < blocks:
@@ -396,6 +401,7 @@
             todo, waiting = todo + white[:share], white[share:]
     for piece in todo:
         piece()
+        send_whitened()
     for copy in rows_out:
         copy.wait()
 

time: 96.7 us -> 101 us (1.044)
  Pallas kernels: 40.7 us -> 45.2 us
  local copies, waits for them, and re-layouts: 2.48 us -> 1.26 us
  other arithmetic: 0.23 us -> 1.31 us
    pallas_call x1, Pallas kernels: 5.8 us -> 8.61 us  [local_gram(): pl.pallas_call(gram_kernel, out_shape=(jax.ShapeDtypeStruct((packed_rows,...]
    unnamed x4, local copies, waits for them, and re-layouts: 2.34 us -> 0.01 us
    pallas_call x1, Pallas kernels: 34.9 us -> 36.5 us  [factor_and_whiten(): pl.pallas_call(factor_kernel, out_shape=(jax.ShapeDtypeStruct((rows, widt...]
    dynamic_slice x1, local copies, waits for them, and re-layouts: 0.06 us -> 1.16 us  [sum_in_pieces(): sent = lax.dynamic_slice_in_dim(packed, (1 - core) * half, half, 0)]
    add x1, other arithmetic: 0.1 us -> 1.18 us  [sum_in_pieces(): piece = kept + lax.ppermute(sent, 'wide', twins)]
where the time goes in v7:
time: 101 us
  blocking collectives  47.5 us (47%)
  Pallas kernels  45.2 us (45%)
  waiting for transfers between devices  4.02 us (4%)
  other arithmetic  1.31 us (1%)
  local copies, waits for them, and re-layouts  1.26 us (1%)
    pallas_call x1, Pallas kernels, factor_and_whiten(): pl.pallas_call(factor_kernel, out_shape=(jax.ShapeDtypeStruct((rows, widt...  36.5 us
    all_to_all x2, blocking collectives, over_grp(): return lax.all_to_all(parts, 'grp', 0, 0)  26.9 us
    all_to_all x2, blocking collectives, over_wide(): return lax.all_to_all(parts, 'wide', 0, 0, axis_index_groups=same_core)  20.6 us
    pallas_call x1, Pallas kernels, local_gram(): pl.pallas_call(gram_kernel, out_shape=(jax.ShapeDtypeStruct((packed_rows,...  8.61 us
    ppermute x1, waiting for transfers between devices, sum_in_pieces(): other = lax.ppermute(held, 'wide', twins)  2.21 us
  transfers between devices with their start and end apart: 2, of which 2 were waited for; matrix products, arithmetic and copies ran while one was open for 0% of the time, Pallas kernels for 0%

profile of v7, /device:TPU:0, one launch (start us, length us, event | category | flops | bytes accessed | tf_op | source)
XLA Modules:
  0.0 100.7 jit_solution(15559265350202432992)
XLA Ops:
  0.6 8.6 %shard_map.41 = (f32[2816,128]{1,0:T(8,128)}, f32[8,128]{1,0:T(8,128)}) custom-call(f32[1536,768]{1,0:T(8,128)} %x_hbm.3), custom_call_target="tpu_custom_call" | custom-call | tf_op jit(solution)/shard_map/pallas_call | solution.py:93
  9.3 1.2 %constant_dynamic-slice_fusion = f32[1408,128]{1,0:T(8,128)S(1)} fusion(f32[2816,128]{1,0:T(8,128)} %get-tuple-element.4, s32[]{:T(128)S(6)} %select_n.7), kind=kLoop, calls=%fused_computation.3 | loop fusion | bytes 1441796 | tf_op jit(solution)/shard_map/dynamic_slice | solution.py:124
  10.4 0.5 collective-permute-start
  10.9 0.0 copy-start.1
  10.9 1.8 %collective-permute-done = f32[1408,128]{1,0:T(8,128)S(1)} collective-permute-done((f32[1408,128]{1,0:T(8,128)S(1)}, f32[1408,128]{1,0:T(8,128)S(1)}, u32[]{:S(2)}, u32[]{:S(2)}) %collective-permute-start) | collective-permute-done | bytes 720928 | tf_op jit(solution)/shard_map/ppermute | solution.py:126
  12.8 1.2 %dynamic-slice_add_fusion = f32[1408,128]{1,0:T(8,128)S(1)} fusion(f32[1408,128]{1,0:T(8,128)S(1)} %collective-permute-done, f32[2816,128]{1,0:T(8,128)} %get-tuple-element.4, s32[]{:T(128)S(6)} %select_n.6), kind=kLoop, calls=%fused_computation | loop fusion | flops 180224 | bytes 2162692 | tf_op jit(solution)/shard_map/add | solution.py:126
  13.9 16.0 %all_to_all.20 = f32[4,352,128]{2,1,0:T(8,128)S(1)} all-to-all(f32[4,352,128]{2,1,0:T(8,128)S(1)} %bitcast.7), channel_id=1, replica_groups=mesh['grp'=4,'wide'=8] {'grp'}, dimensions={0} | all-to-all | bytes 1441792 | tf_op jit(solution)/shard_map/all_to_all | solution.py:115
  29.9 0.0 copy-start
  30.0 11.4 %all_to_all.21 = f32[4,88,128]{2,1,0:T(8,128)S(1)} all-to-all(f32[4,88,128]{2,1,0:T(8,128)S(1)} %bitcast.8), channel_id=1, replica_groups={{0,2,4,6},{1,3,5,7},{8,10,12,14},{9,11,13,15},{16,18,20,22},{17,19,21,2..., dimensions={0} | all-to-all | bytes 360448 | tf_op jit(solution)/shard_map/all_to_all | solution.py:118
  41.4 0.0 copy-done.1
  41.5 9.2 %all_to_all.22 = f32[4,96,128]{2,1,0:T(8,128)S(1)} all-to-all(f32[4,96,128]{2,1,0:T(8,128)S(1)} %broadcast_in_dim.4), channel_id=1, replica_groups={{0,2,4,6},{1,3,5,7},{8,10,12,14},{9,11,13,15},{16,18,20,22},{17,19,21,2..., dimensions={0} | all-to-all | bytes 393216 | tf_op jit(solution)/shard_map/all_to_all | solution.py:118
  50.6 0.1 broadcast_in_dim.5
  50.7 10.9 %all_to_all.23 = f32[4,4,96,128]{3,2,1,0:T(8,128)S(1)} all-to-all(f32[4,4,96,128]{3,2,1,0:T(8,128)S(1)} %broadcast_in_dim.5), channel_id=1, replica_groups=mesh['grp'=4,'wide'=8] {'grp'}, dimensions={0} | all-to-all | bytes 1572864 | tf_op jit(solution)/shard_map/all_to_all | solution.py:115
  61.7 0.0 collective-permute-start.1
  61.7 0.1 pad_add_fusion.numbers_ref
  61.7 2.2 %collective-permute-done.1.other_ref = f32[16,96,128]{2,1,0:T(8,128)S(1)} collective-permute-done((f32[16,96,128]{2,1,0:T(8,128)S(1)}, f32[16,96,128]{2,1,0:T(8,128)S(1)}, u32[]{:S(2)}, u32[]{:S(2)}) %collective-permute-start.1) | collective-permute-done | bytes 786464 | tf_op jit(solution)/shard_map/ppermute | solution.py:133
  63.9 0.0 copy-done
  63.9 36.5 %shard_map.42 = (f32[1536,768]{1,0:T(8,128)}, f32[768,768]{1,0:T(8,128)}) custom-call(f32[1536,768]{1,0:T(8,128)} %x_hbm.3, f32[16,96,128]{2,1,0:T(8,128)S(1)} %bitcast.6, f32[16,96,128]{2,1,0:T(8,128)S(1)} %collective-permute-done.1.other_ref, s32[2]{0:T(128)S(1)} %pad_add_fusion.numbers_ref, f32[2]{0:T(128)S(1)} %copy-done), custom_call_target="tpu_custom_call" | custom-call | tf_op jit(solution)/shard_map/pallas_call | solution.py:417
  (4 shorter events, 0.1 us)
Async XLA Ops:
  10.4 2.3 %collective-permute-start = (f32[1408,128]{1,0:T(8,128)S(1)}, f32[1408,128]{1,0:T(8,128)S(1)}, u32[]{:S(2)}, u32[]{:S(2)}) collective-permute-start(f32[1408,128]{1,0:T(8,128)S(1)} %constant_dynamic-slice_fusion), channel_id=1, source_target_pairs={{0,1},{1,0},{2,3},{3,2},{4,5},{5,4},{6,7},{7,6},{8,9},{9,8},{10,11... | collective-permute-start | bytes 2162696 | tf_op jit(solution)/shard_map/ppermute | solution.py:126
  10.9 30.5 %copy-start.1 = (f32[8,128]{1,0:T(8,128)S(1)}, f32[8,128]{1,0:T(8,128)}, u32[]{:S(2)}) copy-start(f32[8,128]{1,0:T(8,128)} %get-tuple-element.5) | copy-start | bytes 12292
  29.9 34.0 %copy-start = (f32[2]{0:T(128)S(1)}, f32[2]{0:T(128)}, u32[]{:S(2)}) copy-start(f32[2]{0:T(128)} %constant.18.clone.count_ref) | copy-start | bytes 28
  61.7 2.3 %collective-permute-start.1 = (f32[16,96,128]{2,1,0:T(8,128)S(1)}, f32[16,96,128]{2,1,0:T(8,128)S(1)}, u32[]{:S(2)}, u32[]{:S(2)}) collective-permute-start(f32[16,96,128]{2,1,0:T(8,128)S(1)} %bitcast.5), channel_id=1, source_target_pairs={{0,1},{1,0},{2,3},{3,2},{4,5},{5,4},{6,7},{7,6},{8,9},{9,8},{10,11... | collective-permute-start | bytes 2359304 | tf_op jit(solution)/shard_map/ppermute | solution.py:133

commit v8 on v6

--- a/solution.py
+++ b/solution.py
@@ -49,15 +49,10 @@
     ]
 
 
-def gram_kernel(x_hbm, packed_ref, mean_ref, x_ref, both_ref, swapped_ref, arrived):
+def gram_kernel(x_ref, packed_ref, mean_ref, both_ref, swapped_ref):
     rows, width = x_ref.shape
-    copies = chunk_copies(x_hbm, x_ref, arrived)
-    for copy in copies:
-        copy.start()
     total = jnp.zeros((SUB, width), jnp.float32)
     for r in range(0, rows, LANES):
-        if r % TILE == 0:
-            copies[r // TILE].wait()
         part = x_ref[r : r + LANES, :]
         for q in range(0, LANES, SUB):
             total = total + part[q : q + SUB, :]
@@ -98,11 +93,9 @@
             jax.ShapeDtypeStruct((packed_rows, LANES), jnp.float32),
             jax.ShapeDtypeStruct((mean_rows, LANES), jnp.float32),
         ),
-        in_specs=[pl.BlockSpec(memory_space=pl.ANY)],
+        in_specs=[pl.BlockSpec(memory_space=pltpu.VMEM)],
         out_specs=(pl.BlockSpec(memory_space=pltpu.VMEM),) * 2,
-        scratch_shapes=[pltpu.VMEM((rows, width), jnp.float32)]
-        + [pltpu.VMEM((2 * rows, width), jnp.bfloat16)] * 2
-        + [pltpu.SemaphoreType.DMA((rows // TILE,))],
+        scratch_shapes=[pltpu.VMEM((2 * rows, width), jnp.bfloat16)] * 2,
         compiler_params=pltpu.CompilerParams(vmem_limit_bytes=48 * 2**20),
     )(embeddings)
 
@@ -140,56 +133,57 @@
 def factor_block(block, upper_ref, inverse_ref):
     groups = LANES // SUB
     tiles = [block[SUB * p : SUB * (p + 1), :] for p in range(groups)]
-    row_at = lax.broadcasted_iota(jnp.int32, (SUB, LANES), 0)
     lane_at = lax.broadcasted_iota(jnp.int32, (SUB, LANES), 1)
-    unit = [
-        jnp.where(lane_at == row_at + SUB * p, 1.0, 0.0).astype(jnp.float32)
-        for p in range(groups)
-    ]
     for g in range(groups):
         base = SUB * g
         ahead = g + 1 < groups
+        own = (lane_at >= base) & (lane_at < base + SUB)
+        at_lane = [lane_at == base + i for i in range(SUB)]
         rows = [over_rows(tiles[g], i) for i in range(SUB)]
         s = {
             (i, j): over_lanes(rows[i], base + j) for i in range(SUB) for j in range(i, SUB)
         }
-        carried = [over_rows(unit[g], i) for i in range(SUB)]
+        rows = [
+            jnp.where(own, jnp.where(at_lane[i], 1.0, 0.0), rows[i]) for i in range(SUB)
+        ]
         if ahead:
             column = [over_lanes(tiles[g + 1], base + i) for i in range(SUB)]
+            tiles[g + 1] = jnp.where(own, 0.0, tiles[g + 1])
         scale = []
         for j in range(SUB):
             r = lax.rsqrt(s[j, j])
             scale.append(r)
-            for k in range(j + 1, SUB):
+            for k in range(j, SUB):
                 s[j, k] = s[j, k] * r
             for k in range(j + 1, SUB):
                 for m in range(k, SUB):
                     s[k, m] = s[k, m] - s[j, k] * s[j, m]
             rows[j] = rows[j] * r
-            carried[j] = carried[j] * r
             for k in range(j + 1, SUB):
                 rows[k] = rows[k] - s[j, k] * rows[j]
-                carried[k] = carried[k] - s[j, k] * carried[j]
             if ahead:
                 column[j] = column[j] * r
                 for k in range(j + 1, SUB):
                     column[k] = column[k] - column[j] * s[j, k]
                 tiles[g + 1] = tiles[g + 1] - column[j] * rows[j]
-                unit[g + 1] = unit[g + 1] - column[j] * carried[j]
-            upper_ref[base + j : base + j + 1, :] = rows[j][:1, :]
-            inverse_ref[base + j : base + j + 1, :] = carried[j][:1, :]
+            inverse_ref[base + j : base + j + 1, :] = rows[j][:1, :]
+            upper = rows[j]
+            for k in range(j, SUB):
+                upper = jnp.where(at_lane[k], s[j, k], upper)
+            upper_ref[base + j : base + j + 1, :] = upper[:1, :]
         if g + 2 < groups:
             for i in reversed(range(SUB)):
                 for k in range(i + 1, SUB):
                     rows[i] = rows[i] - s[i, k] * rows[k]
-                    carried[i] = carried[i] - s[i, k] * carried[k]
                 rows[i] = rows[i] * scale[i]
-                carried[i] = carried[i] * scale[i]
         for p in range(g + 2, groups):
             column = [over_lanes(tiles[p], base + i) for i in range(SUB)]
-            tiles[p] = tiles[p] - tree_sum([c * x for c, x in zip(column, rows)])
-            unit[p] = unit[p] - tree_sum([c * x for c, x in zip(column, carried)])
+            change = tree_sum([c * x for c, x in zip(column, rows)])
+            tiles[p] = jnp.where(own, 0.0, tiles[p]) - change
         yield
+    row_group = lax.broadcasted_iota(jnp.int32, (LANES, LANES), 0) // SUB
+    lane_group = lax.broadcasted_iota(jnp.int32, (LANES, LANES), 1) // SUB
+    inverse_ref[...] = jnp.where(lane_group <= row_group, inverse_ref[...], 0.0)
 
 
 def tree_sum(terms):

time: 96.7 us -> 96.5 us (level)
  no operation moved by 1% of the time
where the time goes in v8:
time: 96.5 us; the launch traced here: 96.2 us
  blocking collectives  47.5 us (49%)
  Pallas kernels  40.5 us (42%)
  waiting for transfers between devices  4.03 us (4%)
  local copies, waits for them, and re-layouts  2.48 us (3%)
    pallas_call x1, Pallas kernels, factor_and_whiten(): pl.pallas_call(factor_kernel, out_shape=(jax.ShapeDtypeStruct((rows, widt...  35.1 us
    all_to_all x2, blocking collectives, over_grp(): return lax.all_to_all(parts, 'grp', 0, 0)  26.9 us
    all_to_all x2, blocking collectives, over_wide(): return lax.all_to_all(parts, 'wide', 0, 0, axis_index_groups=same_core)  20.6 us
    pallas_call x1, Pallas kernels, local_gram(): pl.pallas_call(gram_kernel, out_shape=(jax.ShapeDtypeStruct((packed_rows,...  5.41 us
    unnamed x4, local copies, waits for them, and re-layouts  2.34 us
    ppermute x1, waiting for transfers between devices, sum_in_pieces(): other = lax.ppermute(held, 'wide', twins)  2.21 us
  transfers between devices with their start and end apart: 2, of which 2 were waited for; matrix products, arithmetic and copies ran while one was open for 0% of the time, Pallas kernels for 0%

profile of v8, /device:TPU:0, one launch (start us, length us, event | category | flops | bytes accessed | tf_op | source)
XLA Modules:
  0.0 96.2 jit_solution(13773127420639905646)
XLA Ops:
  0.6 0.0 copy-start
  0.6 2.3 %copy-done = f32[1536,768]{1,0:T(8,128)S(1)} copy-done((f32[1536,768]{1,0:T(8,128)S(1)}, f32[1536,768]{1,0:T(8,128)}, u32[]{:S(2)}) %copy-start) | copy-done | bytes 4718616
  3.0 5.4 %shard_map.41 = (f32[2816,128]{1,0:T(8,128)S(1)}, f32[8,128]{1,0:T(8,128)S(1)}) custom-call(f32[1536,768]{1,0:T(8,128)S(1)} %copy-done), custom_call_target="tpu_custom_call" | custom-call | tf_op jit(solution)/shard_map/pallas_call | solution.py:90
  8.4 0.1 constant_dynamic-slice_fusion
  8.5 0.5 collective-permute-start
  9.0 1.8 %collective-permute-done = f32[1408,128]{1,0:T(8,128)S(1)} collective-permute-done((f32[1408,128]{1,0:T(8,128)S(1)}, f32[1408,128]{1,0:T(8,128)S(1)}, u32[]{:S(2)}, u32[]{:S(2)}) %collective-permute-start) | collective-permute-done | bytes 720928 | tf_op jit(solution)/shard_map/ppermute | solution.py:121
  10.8 0.1 dynamic-slice_add_fusion
  10.9 16.0 %all_to_all.20 = f32[4,352,128]{2,1,0:T(8,128)S(1)} all-to-all(f32[4,352,128]{2,1,0:T(8,128)S(1)} %bitcast.7), channel_id=1, replica_groups=mesh['grp'=4,'wide'=8] {'grp'}, dimensions={0} | all-to-all | bytes 1441792 | tf_op jit(solution)/shard_map/all_to_all | solution.py:110
  26.9 0.0 copy-start.1
  26.9 11.4 %all_to_all.21 = f32[4,88,128]{2,1,0:T(8,128)S(1)} all-to-all(f32[4,88,128]{2,1,0:T(8,128)S(1)} %bitcast.8), channel_id=1, replica_groups={{0,2,4,6},{1,3,5,7},{8,10,12,14},{9,11,13,15},{16,18,20,22},{17,19,21,2..., dimensions={0} | all-to-all | bytes 360448 | tf_op jit(solution)/shard_map/all_to_all | solution.py:113
  38.4 9.2 %all_to_all.22 = f32[4,96,128]{2,1,0:T(8,128)S(1)} all-to-all(f32[4,96,128]{2,1,0:T(8,128)S(1)} %broadcast_in_dim.4), channel_id=1, replica_groups={{0,2,4,6},{1,3,5,7},{8,10,12,14},{9,11,13,15},{16,18,20,22},{17,19,21,2..., dimensions={0} | all-to-all | bytes 393216 | tf_op jit(solution)/shard_map/all_to_all | solution.py:113
  47.6 0.1 broadcast_in_dim.5
  47.7 10.9 %all_to_all.23 = f32[4,4,96,128]{3,2,1,0:T(8,128)S(1)} all-to-all(f32[4,4,96,128]{3,2,1,0:T(8,128)S(1)} %broadcast_in_dim.5), channel_id=1, replica_groups=mesh['grp'=4,'wide'=8] {'grp'}, dimensions={0} | all-to-all | bytes 1572864 | tf_op jit(solution)/shard_map/all_to_all | solution.py:110
  58.6 0.0 collective-permute-start.1
  58.6 0.1 pad_add_fusion.numbers_ref
  58.7 2.2 %collective-permute-done.1.other_ref = f32[16,96,128]{2,1,0:T(8,128)S(1)} collective-permute-done((f32[16,96,128]{2,1,0:T(8,128)S(1)}, f32[16,96,128]{2,1,0:T(8,128)S(1)}, u32[]{:S(2)}, u32[]{:S(2)}) %collective-permute-start.1) | collective-permute-done | bytes 786464 | tf_op jit(solution)/shard_map/ppermute | solution.py:128
  60.9 0.0 copy-done.1
  60.9 35.1 %shard_map.42 = (f32[1536,768]{1,0:T(8,128)}, f32[768,768]{1,0:T(8,128)}) custom-call(f32[1536,768]{1,0:T(8,128)} %x_hbm.1, f32[16,96,128]{2,1,0:T(8,128)S(1)} %bitcast.6, f32[16,96,128]{2,1,0:T(8,128)S(1)} %collective-permute-done.1.other_ref, s32[2]{0:T(128)S(1)} %pad_add_fusion.numbers_ref, f32[2]{0:T(128)S(1)} %copy-done.1), custom_call_target="tpu_custom_call" | custom-call | tf_op jit(solution)/shard_map/pallas_call | solution.py:405
  (4 shorter events, 0.1 us)
Async XLA Ops:
  0.6 2.3 %copy-start = (f32[1536,768]{1,0:T(8,128)S(1)}, f32[1536,768]{1,0:T(8,128)}, u32[]{:S(2)}) copy-start(f32[1536,768]{1,0:T(8,128)} %x_hbm.1) | copy-start | bytes 14155780
  8.5 2.3 %collective-permute-start = (f32[1408,128]{1,0:T(8,128)S(1)}, f32[1408,128]{1,0:T(8,128)S(1)}, u32[]{:S(2)}, u32[]{:S(2)}) collective-permute-start(f32[1408,128]{1,0:T(8,128)S(1)} %constant_dynamic-slice_fusion), channel_id=1, source_target_pairs={{0,1},{1,0},{2,3},{3,2},{4,5},{5,4},{6,7},{7,6},{8,9},{9,8},{10,11... | collective-permute-start | bytes 2162696 | tf_op jit(solution)/shard_map/ppermute | solution.py:121
  26.9 34.0 %copy-start.1 = (f32[2]{0:T(128)S(1)}, f32[2]{0:T(128)}, u32[]{:S(2)}) copy-start(f32[2]{0:T(128)} %constant.18.clone.count_ref) | copy-start | bytes 28
  58.6 2.3 %collective-permute-start.1 = (f32[16,96,128]{2,1,0:T(8,128)S(1)}, f32[16,96,128]{2,1,0:T(8,128)S(1)}, u32[]{:S(2)}, u32[]{:S(2)}) collective-permute-start(f32[16,96,128]{2,1,0:T(8,128)S(1)} %bitcast.5), channel_id=1, source_target_pairs={{0,1},{1,0},{2,3},{3,2},{4,5},{5,4},{6,7},{7,6},{8,9},{9,8},{10,11... | collective-permute-start | bytes 2359304 | tf_op jit(solution)/shard_map/ppermute | solution.py:128

commit v9 on v4

--- a/solution.py
+++ b/solution.py
@@ -271,9 +271,9 @@
                 factor = jnp.where(col_at >= row_at, upper_ref[k % 2], 0.0)
                 back = inverse_ref[k % 2]
             factor_ref[span(k), span(j)] = factor * (1.0 / total_scale)
-            high, low = split(back * total_scale)
-            high_ref[span(k), span(j)] = high
-            low_ref[span(k), span(j)] = low
+            high, low = split((back * total_scale).T)
+            high_ref[span(j), span(k)] = high
+            low_ref[span(j), span(k)] = low
 
     def below(k, i, left, right, first):
         change = parts_dot(left, [r[:, : LANES * (k + 1)] for r in right])
@@ -377,9 +377,9 @@
     for right in range(0, width, TILE):
         here = slice(right, right + TILE)
         deep = slice(0, right + TILE)
-        tile = fast_dot(high[:, deep], high_ref[here, deep], ((1,), (1,)))
-        tile = tile + fast_dot(high[:, deep], low_ref[here, deep], ((1,), (1,)))
-        out_ref[:, here] = tile + fast_dot(low[:, deep], high_ref[here, deep], ((1,), (1,)))
+        tile = fast_dot(high[:, deep], high_ref[deep, here], ((1,), (0,)))
+        tile = tile + fast_dot(high[:, deep], low_ref[deep, here], ((1,), (0,)))
+        out_ref[:, here] = tile + fast_dot(low[:, deep], high_ref[deep, here], ((1,), (0,)))
 
 
 def whiten(embeddings, mean, high, low):

time: 97.7 us -> 96.6 us (0.989)
  Pallas kernels: 41.8 us -> 40.7 us
where the time goes in v9:
time: 96.6 us; the launch traced here: 96.2 us
  blocking collectives  47.5 us (49%)
  Pallas kernels  40.7 us (42%)
  waiting for transfers between devices  4.03 us (4%)
  local copies, waits for them, and re-layouts  2.48 us (3%)
    pallas_call x1, Pallas kernels, factor_and_inverse(): pl.pallas_call(factor_kernel, out_shape=(jax.ShapeDtypeStruct((width, wid...  27.1 us
    all_to_all x2, blocking collectives, over_grp(): return lax.all_to_all(parts, 'grp', 0, 0)  26.9 us
    all_to_all x2, blocking collectives, over_wide(): return lax.all_to_all(parts, 'wide', 0, 0, axis_index_groups=same_core)  20.6 us
    pallas_call x1, Pallas kernels, whiten(): pl.pallas_call(whiten_kernel, grid=(rows // TILE,), out_shape=jax.ShapeDt...  8.17 us
    pallas_call x1, Pallas kernels, local_gram(): pl.pallas_call(gram_kernel, out_shape=(jax.ShapeDtypeStruct((packed_rows,...  5.41 us
    unnamed x4, local copies, waits for them, and re-layouts  2.34 us
    ppermute x1, waiting for transfers between devices, sum_in_pieces(): other = lax.ppermute(held, 'wide', twins)  2.21 us
  transfers between devices with their start and end apart: 2, of which 2 were waited for; matrix products, arithmetic and copies ran while one was open for 0% of the time, Pallas kernels for 0%

profile of v9, /device:TPU:0, one launch (start us, length us, event | category | flops | bytes accessed | tf_op | source)
XLA Modules:
  0.0 96.2 jit_solution(6664677454055497948)
XLA Ops:
  0.6 0.0 copy-start
  0.6 2.3 %copy-done = f32[1536,768]{1,0:T(8,128)S(1)} copy-done((f32[1536,768]{1,0:T(8,128)S(1)}, f32[1536,768]{1,0:T(8,128)}, u32[]{:S(2)}) %copy-start) | copy-done | bytes 4718616
  3.0 5.4 %shard_map.41 = (f32[2816,128]{1,0:T(8,128)S(1)}, f32[8,128]{1,0:T(8,128)S(1)}) custom-call(f32[1536,768]{1,0:T(8,128)S(1)} %copy-done), custom_call_target="tpu_custom_call" | custom-call | tf_op jit(solution)/shard_map/pallas_call | solution.py:81
  8.4 0.1 constant_dynamic-slice_fusion
  8.5 0.5 collective-permute-start
  9.0 1.8 %collective-permute-done = f32[1408,128]{1,0:T(8,128)S(1)} collective-permute-done((f32[1408,128]{1,0:T(8,128)S(1)}, f32[1408,128]{1,0:T(8,128)S(1)}, u32[]{:S(2)}, u32[]{:S(2)}) %collective-permute-start) | collective-permute-done | bytes 720928 | tf_op jit(solution)/shard_map/ppermute | solution.py:112
  10.8 0.1 dynamic-slice_add_fusion
  10.9 16.0 %all_to_all.20 = f32[4,352,128]{2,1,0:T(8,128)S(1)} all-to-all(f32[4,352,128]{2,1,0:T(8,128)S(1)} %bitcast.7), channel_id=1, replica_groups=mesh['grp'=4,'wide'=8] {'grp'}, dimensions={0} | all-to-all | bytes 1441792 | tf_op jit(solution)/shard_map/all_to_all | solution.py:101
  26.9 11.4 %all_to_all.21 = f32[4,88,128]{2,1,0:T(8,128)S(1)} all-to-all(f32[4,88,128]{2,1,0:T(8,128)S(1)} %bitcast.8), channel_id=1, replica_groups={{0,2,4,6},{1,3,5,7},{8,10,12,14},{9,11,13,15},{16,18,20,22},{17,19,21,2..., dimensions={0} | all-to-all | bytes 360448 | tf_op jit(solution)/shard_map/all_to_all | solution.py:104
  38.4 0.0 copy-start.1
  38.4 9.2 %all_to_all.22 = f32[4,96,128]{2,1,0:T(8,128)S(1)} all-to-all(f32[4,96,128]{2,1,0:T(8,128)S(1)} %broadcast_in_dim.4), channel_id=1, replica_groups={{0,2,4,6},{1,3,5,7},{8,10,12,14},{9,11,13,15},{16,18,20,22},{17,19,21,2..., dimensions={0} | all-to-all | bytes 393216 | tf_op jit(solution)/shard_map/all_to_all | solution.py:104
  47.6 0.1 broadcast_in_dim.5
  47.7 10.9 %all_to_all.23 = f32[4,4,96,128]{3,2,1,0:T(8,128)S(1)} all-to-all(f32[4,4,96,128]{3,2,1,0:T(8,128)S(1)} %broadcast_in_dim.5), channel_id=1, replica_groups=mesh['grp'=4,'wide'=8] {'grp'}, dimensions={0} | all-to-all | bytes 1572864 | tf_op jit(solution)/shard_map/all_to_all | solution.py:101
  58.6 0.0 collective-permute-start.1
  58.6 0.1 pad_add_fusion.numbers_ref
  58.7 2.2 %collective-permute-done.1.other_ref = f32[16,96,128]{2,1,0:T(8,128)S(1)} collective-permute-done((f32[16,96,128]{2,1,0:T(8,128)S(1)}, f32[16,96,128]{2,1,0:T(8,128)S(1)}, u32[]{:S(2)}, u32[]{:S(2)}) %collective-permute-start.1) | collective-permute-done | bytes 786464 | tf_op jit(solution)/shard_map/ppermute | solution.py:119
  60.9 0.0 copy-done.1
  60.9 27.1 %shard_map.42 = (f32[768,768]{1,0:T(8,128)}, bf16[768,768]{1,0:T(8,128)(2,1)S(1)}, bf16[768,768]{1,0:T(8,128)(2,1)S(1)}, f32[8,768]{1,0:T(8,128)S(1)}) custom-call(f32[16,96,128]{2,1,0:T(8,128)S(1)} %bitcast.6, f32[16,96,128]{2,1,0:T(8,128)S(1)} %collective-permute-done.1.other_ref, s32[2]{0:T(128)S(1)} %pad_add_fusion.numbers_ref, f32[2]{0:T(128)S(1)} %copy-done.1), custom_call_target="tpu_custom_call" | custom-call | tf_op jit(solution)/shard_map/pallas_call | solution.py:353
  88.0 8.2 %shard_map.43 = f32[1536,768]{1,0:T(8,128)} custom-call(f32[1536,768]{1,0:T(8,128)} %x_ref.3, f32[8,768]{1,0:T(8,128)S(1)} %get-tuple-element.10.mean_ref, bf16[768,768]{1,0:T(8,128)(2,1)S(1)} %get-tuple-element.11.high_ref, bf16[768,768]{1,0:T(8,128)(2,1)S(1)} %get-tuple-element.12.low_ref), custom_call_target="tpu_custom_call" | custom-call | tf_op jit(solution)/shard_map/pallas_call | solution.py:388
  (4 shorter events, 0.1 us)
Async XLA Ops:
  0.6 2.3 %copy-start = (f32[1536,768]{1,0:T(8,128)S(1)}, f32[1536,768]{1,0:T(8,128)}, u32[]{:S(2)}) copy-start(f32[1536,768]{1,0:T(8,128)} %x_ref.3) | copy-start | bytes 14155780
  8.5 2.3 %collective-permute-start = (f32[1408,128]{1,0:T(8,128)S(1)}, f32[1408,128]{1,0:T(8,128)S(1)}, u32[]{:S(2)}, u32[]{:S(2)}) collective-permute-start(f32[1408,128]{1,0:T(8,128)S(1)} %constant_dynamic-slice_fusion), channel_id=1, source_target_pairs={{0,1},{1,0},{2,3},{3,2},{4,5},{5,4},{6,7},{7,6},{8,9},{9,8},{10,11... | collective-permute-start | bytes 2162696 | tf_op jit(solution)/shard_map/ppermute | solution.py:112
  38.4 22.5 %copy-start.1 = (f32[2]{0:T(128)S(1)}, f32[2]{0:T(128)}, u32[]{:S(2)}) copy-start(f32[2]{0:T(128)} %constant.18.clone.count_ref) | copy-start | bytes 28
  58.6 2.3 %collective-permute-start.1 = (f32[16,96,128]{2,1,0:T(8,128)S(1)}, f32[16,96,128]{2,1,0:T(8,128)S(1)}, u32[]{:S(2)}, u32[]{:S(2)}) collective-permute-start(f32[16,96,128]{2,1,0:T(8,128)S(1)} %bitcast.5), channel_id=1, source_target_pairs={{0,1},{1,0},{2,3},{3,2},{4,5},{5,4},{6,7},{7,6},{8,9},{9,8},{10,11... | collective-permute-start | bytes 2359304 | tf_op jit(solution)/shard_map/ppermute | solution.py:119
